TPU v7x, 512 devices: a whole 4x4x16 slice. The times are simulated.
512 devices in a mesh: row: 32 (over x, y, core), col: 16 (over z).
Axes of the slice: x: 4, y: 4, z: 16, core: 2. Of those that a mesh axis runs over, the one named last changes fastest.
Arguments:
- momentum: bfloat16 [8192, 28672], P('row', 'col'), may hold values from -120 to 120
- gradient: bfloat16 [8192, 28672], P('row', 'col'), may hold values from -6 to 6
- right_factor: bfloat16 [28672, 256], P('col'), may hold values from -0.03125 to 0.03125
Outputs:
- new_momentum: bfloat16 [8192, 28672], P('row', 'col')
- new_right: bfloat16 [28672, 256], P('col')
- left_factor: float32 [8192, 256], P('row')
All inputs are finite; a program needn't handle non-finite values.
Results may differ from a plain program's by a relative error of at most 0.013.
Values sent between devices are 32-bit elements; how exact they have to be, the bound alone decides.
No kernel may reach another device: no remote copies, remote signals or barrier semaphores. Data moves between devices by JAX's collectives and lax.ppermute only.
A program may use at most 64 MiB of HBM per device.

v0:
```python
import jax
import jax.numpy as jnp
from jax import lax
from jax.sharding import PartitionSpec as P


def local(momentum, gradient, right_factor):
    blend = (momentum.astype(jnp.float32) + gradient.astype(jnp.float32)).astype(jnp.bfloat16)
    left = lax.psum(jnp.dot(blend, right_factor, preferred_element_type=jnp.float32), "col")
    gram = lax.psum(jnp.dot(left.T, left, precision=lax.Precision.HIGHEST), "row")
    lower = jnp.linalg.cholesky(gram)
    left_factor = lax.linalg.triangular_solve(
        lower, left, left_side=False, lower=True, transpose_a=True
    )
    ortho_b = left_factor.astype(jnp.bfloat16)
    partial_right = lax.dot_general(
        blend, ortho_b, (((0,), (0,)), ((), ())), preferred_element_type=jnp.float32
    )
    right = lax.psum(partial_right, "row")
    total = lax.psum(jnp.sum(right * right, axis=0), "col")
    new_right = (right * lax.rsqrt(total + 1e-08)).astype(jnp.bfloat16)
    right_b = right.astype(jnp.bfloat16)
    correction = lax.dot_general(
        ortho_b, right_b, (((1,), (1,)), ((), ())), preferred_element_type=jnp.float32
    )
    new_momentum = (blend.astype(jnp.float32) - 0.1 * correction).astype(jnp.bfloat16)
    return (new_momentum, new_right, left_factor)


def solution(mesh):
    placed = (P("row", "col"), P("row", "col"), P("col", None))
    return jax.shard_map(
        local,
        mesh=mesh,
        in_specs=placed,
        out_specs=(P("row", "col"), P("col", None), P("row", None)),
        check_vma=False,
    )
```

profile of v0, /device:TPU:1, one launch (start us, length us, event | category | flops | bytes accessed | tf_op | source)
XLA Modules:
  0.0 528.4 jit_solution(7996763748906984000)
XLA Ops:
  7.2 1.1 copy-done
  8.3 2.6 fusion.14
  11.0 131.7 %all-reduce.5.cloned.1.call-done = f32[256,256]{1,0:T(8,128)} async-done(((f32[256,256]{1,0:T(8,128)}), f32[256,256]{1,0:T(8,128)}) %all-reduce.5.cloned.1.call-update) | async-done | bytes 262160 | tf_op jit(solution)/shard_map/psum | solution.py:9
  142.7 2.3 fusion.16
  145.1 139.8 %all-reduce.7.cloned.1.call-done = f32[256,256]{0,1:T(8,128)} async-done(((f32[256,256]{0,1:T(8,128)}), f32[256,256]{0,1:T(8,128)}) %all-reduce.7.cloned.1.call-update) | async-done | bytes 262160 | tf_op jit(solution)/shard_map/psum | solution.py:10
  284.9 1.1 copy.7
  286.0 1.0 fusion.3
  287.1 0.7 copy-done.6
  287.8 11.7 %cholesky.50 = f32[128,128]{1,0:T(8,128)S(1)} custom-call(f32[128,128]{1,0:T(8,128)S(1)} %cholesky.118), custom_call_target="Cholesky" | custom-call | tf_op jit(solution)/shard_map/jit(cholesky)/cholesky | solution.py:11
  299.5 9.8 %custom-call.14 = f32[1,128,128]{1,2,0:T(8,128)S(1)} custom-call(f32[1,128,128]{2,1,0:T(8,128)S(1)} %get-tuple-element.27), custom_call_target="InvertDiagBlocksLowerTriangular" | custom-call | tf_op jit(solution)/shard_map/jit(cholesky)/cholesky | solution.py:11
  309.4 1.0 constant_dynamic-update-slice_fusion.1
  310.4 1.1 convolution_subtract_fusion.1
  311.5 11.7 %cholesky.105 = f32[128,128]{1,0:T(8,128)S(1)} custom-call(f32[128,128]{1,0:T(8,128)S(1)} %convolution_subtract_fusion.1), custom_call_target="Cholesky" | custom-call | tf_op jit(solution)/shard_map/jit(cholesky)/cholesky | solution.py:11
  323.3 0.7 compare_reduce_fusion
  325.2 1.0 select_select_fusion
  326.2 0.1 triangular_solve.58
  326.3 5.3 %while.1 = (s32[]{:T(128)}, f32[256,256]{1,0:T(8,128)S(1)}, s32[2,2]{1,0:T(2,128)S(1)}, f32[2,128,128]{2,1,0:T(8,128)}, s32[]{:T(128)}) while((s32[]{:T(128)}, f32[256,256]{1,0:T(8,128)S(1)}, s32[2,2]{1,0:T(2,128)S(1)}, f32[2,128,128]{2,1,0:T(8,128)}, s32[]{:T(128)}) %tuple.28), condition=%wide.while_cond, body=%wide.while_body.sunk | while | flops 2 | bytes 132205 | solution.py:12
  326.4 0.6 fusion.25
  327.0 2.0 bitcast_dynamic-update-slice_fusion.2
  329.0 0.6 fusion.25
  329.6 2.0 bitcast_dynamic-update-slice_fusion.2
  331.6 20.5 %custom-call.15 = f32[2,128,128]{1,2,0:T(8,128)S(1)} custom-call(f32[2,128,128]{2,1,0:T(8,128)} %get-tuple-element.10), custom_call_target="InvertDiagBlocksLowerTriangular" | custom-call | tf_op jit(solution)/shard_map/triangular_solve | solution.py:12
  352.1 0.3 fusion.4
  352.4 0.4 convolution_subtract_fusion
  352.8 0.3 fusion.6
  353.2 1.7 fusion.12
  354.9 0.8 copy.8
  355.7 135.9 %all-reduce.9.cloned.1.call-done = f32[1792,256]{1,0:T(8,128)} async-done(((f32[1792,256]{1,0:T(8,128)}), f32[1792,256]{1,0:T(8,128)}) %all-reduce.9.cloned.1.call-update) | async-done | bytes 1835024 | tf_op jit(solution)/shard_map/psum | solution.py:19
  491.7 1.9 multiply_reduce_fusion
  493.6 24.3 %psum.31 = f32[256]{0:T(256)S(1)} all-reduce(f32[256]{0:T(256)S(1)} %multiply_reduce_fusion), channel_id=1, replica_groups=mesh['row'=32,'col'=16] {'col'}, use_global_device_ids=true, to_apply=%region_8.9 | all-reduce | flops 256 | bytes 2048 | tf_op jit(solution)/shard_map/psum | solution.py:20
  517.9 2.9 fusion.1
  520.8 1.1 multiply_convert_fusion
  (28 shorter events, 0.3 us)
Async XLA Ops:
  7.2 1.2 copy-start
  7.2 135.5 %all-reduce.5.cloned.1.call-start = ((), (), s32[]{:S(2)}) async-start(), calls=%async_computation | async-start | bytes 524288 | tf_op jit(solution)/shard_map/psum | solution.py:9
  10.9 274.0 %all-reduce.7.cloned.1.call-start = ((), (), s32[]{:S(2)}) async-start(), calls=%async_computation.1 | async-start | bytes 524288 | tf_op jit(solution)/shard_map/psum | solution.py:10
  145.0 346.7 %all-reduce.9.cloned.1.call-start = ((), (), s32[]{:S(2)}) async-start(), calls=%async_computation.2 | async-start | bytes 3670016 | tf_op jit(solution)/shard_map/psum | solution.py:19
  286.0 66.1 %copy-start.4 = (f32[256,256]{1,0:T(8,128)S(1)}, f32[256,256]{1,0:T(8,128)}, u32[]{:S(2)}) copy-start(f32[256,256]{1,0:T(8,128)} %all-reduce.5.cloned.1.call-done) | copy-start | bytes 786436
  287.0 0.7 copy-start.6
  287.8 65.4 %copy-start.2 = (bf16[256,1792]{1,0:T(8,128)(2,1)S(1)}, bf16[256,1792]{1,0:T(8,128)(2,1)}, u32[]{:S(2)}) copy-start(bf16[256,1792]{1,0:T(8,128)(2,1)} %param.4) | copy-start | bytes 2752516
  287.8 65.4 %copy-start.3 = (bf16[256,1792]{1,0:T(8,128)(2,1)S(1)}, bf16[256,1792]{1,0:T(8,128)(2,1)}, u32[]{:S(2)}) copy-start(bf16[256,1792]{1,0:T(8,128)(2,1)} %param.3) | copy-start | bytes 2752516
  323.3 2.0 copy-start.5
  491.7 26.2 %copy-start.1 = (f32[1792,256]{1,0:T(8,128)S(1)}, f32[1792,256]{1,0:T(8,128)}, u32[]{:S(2)}) copy-start(f32[1792,256]{1,0:T(8,128)} %all-reduce.9.cloned.1.call-done) | copy-start | bytes 5505028
Sparse Core Ops, SparseCore 0:
  11.1 131.5 all-reduce.4
  146.8 138.0 all-reduce.6
  355.0 136.6 all-reduce.8
where the time goes:
time: 536 us; the launch traced here: 528 us
  waiting for transfers between devices  407 us (76%)
  other arithmetic  59.5 us (11%)
  blocking collectives  24.3 us (5%)
  between operations  15.2 us (3%)
  matrix products  12.7 us (2%)
  local copies, waits for them, and re-layouts  9.02 us (2%)
    psum x1, waiting for transfers between devices, local(): lax.psum(jnp.dot(left.T, left, precision=lax.Precision.HIGHEST), 'row')  140 us
    psum x1, waiting for transfers between devices, local(): right = lax.psum(partial_right, 'row')  136 us
    psum x1, waiting for transfers between devices, local(): lax.psum(jnp.dot(blend, right_factor, preferred_element_type=jnp.float32)...  132 us
    another operation x6, other arithmetic, local(): lower = jnp.linalg.cholesky(gram)  34 us
    psum x1, blocking collectives, local(): total = lax.psum(jnp.sum(right * right, axis=0), 'col')  24.3 us
    another operation x4, other arithmetic, local(): lax.linalg.triangular_solve(lower, left, left_side=False, lower=True, tra...  21.5 us
  transfers between devices with their start and end apart: 3, of which 3 were waited for; matrix products, arithmetic and copies ran while one was open for 0% of the time, Pallas kernels for 0%

commit v1 on v0

v1 whole, which is shorter than its diff:
```python
import jax
import jax.numpy as jnp
from jax import lax
from jax.sharding import PartitionSpec as P

ROWS = 32
COLS = 16
HIGHEST = lax.Precision.HIGHEST
SAME_CORE = [[2 * chip + core for chip in range(ROWS // 2)] for core in range(2)]
SIBLINGS = [(index, index ^ 1) for index in range(ROWS)]


def scatter_sum(x, axis, count, groups=None):
    moved = lax.all_to_all(x, axis, 0, 0, axis_index_groups=groups, tiled=True)
    return jnp.sum(moved.reshape(count, x.shape[0] // count, x.shape[1]), axis=0)


def gather(x, axis, count, groups=None):
    copies = jnp.broadcast_to(x[None], (count,) + x.shape).reshape(count * x.shape[0], x.shape[1])
    return lax.all_to_all(copies, axis, 0, 0, axis_index_groups=groups, tiled=True)


def split3(x):
    first = lax.reduce_precision(x, 8, 7)
    rest = x - first
    second = lax.reduce_precision(rest, 8, 7)
    third = rest - second
    return first.astype(jnp.bfloat16), second.astype(jnp.bfloat16), third.astype(jnp.bfloat16)


def row_sum_large(x):
    core = lax.axis_index("row") % 2
    half = x.shape[0] // 2
    other = lax.dynamic_slice_in_dim(x, (1 - core) * half, half, 0)
    mine = lax.dynamic_slice_in_dim(x, core * half, half, 0)
    mine = mine + lax.ppermute(other, "row", SIBLINGS)
    piece = scatter_sum(mine, "row", ROWS // 2, SAME_CORE)
    mine = gather(piece, "row", ROWS // 2, SAME_CORE)
    other = lax.ppermute(mine, "row", SIBLINGS)
    first = jnp.where(core == 0, mine, other)
    second = jnp.where(core == 0, other, mine)
    return jnp.concatenate([first, second], axis=0)


def local(momentum, gradient, right_factor):
    blend = (momentum.astype(jnp.float32) + gradient.astype(jnp.float32)).astype(jnp.bfloat16)
    left = jnp.dot(blend, right_factor, preferred_element_type=jnp.float32)
    left = gather(scatter_sum(left, "col", COLS), "col", COLS)
    gram = jnp.dot(left.T, left, precision=HIGHEST)
    gram = gather(scatter_sum(gram, "row", ROWS), "row", ROWS)
    product = sum(
        lax.dot_general(blend, term, (((0,), (0,)), ((), ())), preferred_element_type=jnp.float32)
        for term in split3(left)
    )
    product = row_sum_large(product)
    lower = jnp.linalg.cholesky(gram)
    inverse = lax.linalg.triangular_solve(lower, jnp.eye(gram.shape[0], dtype=jnp.float32), left_side=True, lower=True)
    left_factor = jnp.dot(left, inverse.T, precision=HIGHEST)
    right = jnp.dot(product, inverse.T, precision=HIGHEST)
    ortho_b = left_factor.astype(jnp.bfloat16)
    sums = jnp.sum(right * right, axis=0, keepdims=True)
    total = jnp.sum(gather(sums, "col", COLS), axis=0)
    new_right = (right * lax.rsqrt(total + 1e-08)).astype(jnp.bfloat16)
    right_b = right.astype(jnp.bfloat16)
    correction = lax.dot_general(
        ortho_b, right_b, (((1,), (1,)), ((), ())), preferred_element_type=jnp.float32
    )
    new_momentum = (blend.astype(jnp.float32) - 0.1 * correction).astype(jnp.bfloat16)
    return (new_momentum, new_right, left_factor)


def solution(mesh):
    placed = (P("row", "col"), P("row", "col"), P("col", None))
    return jax.shard_map(
        local,
        mesh=mesh,
        in_specs=placed,
        out_specs=(P("row", "col"), P("col", None), P("row", None)),
        check_vma=False,
    )
```

time: 536 us -> 209 us (0.39); the launches traced: 528 us -> 208 us
  waiting for transfers between devices: 407 us -> 30 us
  starting transfers between devices: 0.12 us -> 41.4 us
  blocking collectives: 24.3 us -> 44.7 us
  between operations: 15.2 us -> 2.33 us
  other arithmetic: 59.5 us -> 66.1 us
    psum x3 -> x0, waiting for transfers between devices: 407 us -> none  [the longest x1 140 us: local(): lax.psum(jnp.dot(left.T, left, precision=lax.Precision.HIGHEST), 'row')]
    all_to_all x0 -> x2, blocking collectives: none -> 44.7 us  [scatter_sum(): moved = lax.all_to_all(x, axis, 0, 0, axis_index_groups=groups, tiled=True)]
    all_to_all x0 -> x5, starting transfers between devices: none -> 30.3 us  [the longest x4 26.5 us: gather(): lax.all_to_all(copies, axis, 0, 0, axis_index_groups=groups, tiled=True)]
    all_to_all x0 -> x5, waiting for transfers between devices: none -> 30 us  [the longest x4 30 us: gather(): lax.all_to_all(copies, axis, 0, 0, axis_index_groups=groups, tiled=True)]
    psum x1 -> x0, blocking collectives: 24.3 us -> none  [local(): total = lax.psum(jnp.sum(right * right, axis=0), 'col')]
    ppermute x0 -> x2, starting transfers between devices: none -> 11.1 us  [the longest x1 8.25 us: row_sum_large(): mine = mine + lax.ppermute(other, 'row', SIBLINGS)]
    another operation x4 -> x3, other arithmetic: 21.5 us -> 20.5 us  [local(): lax.linalg.triangular_solve(lower, jnp.eye(gram.shape[0], dtype=jnp.float...]
  transfers between devices with their start and end apart: 3 -> 7, of which waited for: 3 -> 3; matrix products, arithmetic and copies ran while one was open for 0% -> 35% of each run, Pallas kernels for 0% -> 0%
where the time goes in v1:
time: 209 us; the launch traced here: 208 us
  other arithmetic  66.1 us (32%)
  blocking collectives  44.7 us (21%)
  starting transfers between devices  41.4 us (20%)
  waiting for transfers between devices  30 us (14%)
  matrix products  12.6 us (6%)
  local copies, waits for them, and re-layouts  11 us (5%)
  between operations  2.33 us (1%)
    all_to_all x2, blocking collectives, scatter_sum(): moved = lax.all_to_all(x, axis, 0, 0, axis_index_groups=groups, tiled=True)  44.7 us
    another operation x6, other arithmetic, local(): lower = jnp.linalg.cholesky(gram)  37.8 us
    all_to_all x4, waiting for transfers between devices, gather(): lax.all_to_all(copies, axis, 0, 0, axis_index_groups=groups, tiled=True)  30 us
    all_to_all x4, starting transfers between devices, gather(): lax.all_to_all(copies, axis, 0, 0, axis_index_groups=groups, tiled=True)  26.5 us
    another operation x3, other arithmetic, local(): lax.linalg.triangular_solve(lower, jnp.eye(gram.shape[0], dtype=jnp.float...  20.5 us
    ppermute x1, starting transfers between devices, row_sum_large(): mine = mine + lax.ppermute(other, 'row', SIBLINGS)  8.25 us
    another operation x6, local copies, waits for them, and re-layouts  5.32 us
  transfers between devices with their start and end apart: 7, of which 3 were waited for; matrix products, arithmetic and copies ran while one was open for 35% of the time, Pallas kernels for 0%

profile of v1, /device:TPU:1, one launch (start us, length us, event | category | flops | bytes accessed | tf_op | source)
XLA Modules:
  0.0 208.1 jit_solution(18094874882409921187)
XLA Ops:
  0.6 1.7 add_convert_fusion
  2.8 28.7 %all_to_all.57 = f32[16,16,256]{2,1,0:T(8,128)S(1)} all-to-all(f32[16,16,256]{2,1,0:T(8,128)S(1)} %bitcast.62), channel_id=1, replica_groups=mesh['row'=32,'col'=16] {'col'}, dimensions={0} | all-to-all | bytes 524288 | tf_op jit(solution)/shard_map/all_to_all | solution.py:14
  32.3 10.9 %all-to-all-start.1 = ((f32[16,16,256]{2,1,0:T(8,128)}), f32[16,16,256]{2,1,0:T(8,128)S(1)}, u32[]{:S(2)}, u32[]{:S(2)}) async-start(f32[16,16,256]{2,1,0:T(8,128)} %broadcast_in_dim.7), calls=%async_computation.1 | async-start | bytes 524288 | tf_op jit(solution)/shard_map/all_to_all | solution.py:20
  43.2 13.0 %all-to-all-done.1 = f32[16,16,256]{2,1,0:T(8,128)S(1)} async-done(((f32[16,16,256]{2,1,0:T(8,128)}), f32[16,16,256]{2,1,0:T(8,128)S(1)}, u32[]{:S(2)}, u32[]{:S(2)}) %all-to-all-start.1) | async-done | bytes 262176 | tf_op jit(solution)/shard_map/all_to_all | solution.py:20
  57.7 1.2 copy-done.1
  58.9 1.0 constant_dynamic-slice_fusion.1
  59.9 8.3 %collective-permute-start = (f32[896,256]{1,0:T(8,128)}, f32[896,256]{1,0:T(8,128)}, u32[]{:S(2)}, u32[]{:S(2)}) collective-permute-start(f32[896,256]{1,0:T(8,128)} %constant_dynamic-slice_fusion.1), channel_id=1, source_target_pairs={{0,16},{16,0},{32,48},{48,32},{64,80},{80,64},{96,112},{112,96},{1... | collective-permute-start | bytes 2752520 | tf_op jit(solution)/shard_map/ppermute | solution.py:36
  68.7 16.0 %all_to_all.58 = f32[32,8,256]{2,1,0:T(8,128)S(1)} all-to-all(f32[32,8,256]{2,1,0:T(8,128)S(1)} %fusion.9), channel_id=1, replica_groups=mesh['row'=32,'col'=16] {'row'}, dimensions={0} | all-to-all | bytes 524288 | tf_op jit(solution)/shard_map/all_to_all | solution.py:14
  85.4 3.7 %all-to-all-start.3 = ((f32[32,8,256]{2,1,0:T(8,128)}), f32[32,8,256]{2,1,0:T(8,128)S(1)}, u32[]{:S(2)}, u32[]{:S(2)}) async-start(f32[32,8,256]{2,1,0:T(8,128)} %broadcast_in_dim.8), calls=%async_computation.3 | async-start | bytes 524288 | tf_op jit(solution)/shard_map/all_to_all | solution.py:20
  89.8 8.4 %all-to-all-done.3 = f32[32,8,256]{2,1,0:T(8,128)S(1)} async-done(((f32[32,8,256]{2,1,0:T(8,128)}), f32[32,8,256]{2,1,0:T(8,128)S(1)}, u32[]{:S(2)}, u32[]{:S(2)}) %all-to-all-start.3) | async-done | bytes 262176 | tf_op jit(solution)/shard_map/all_to_all | solution.py:20
  98.4 11.7 %cholesky.50 = f32[128,128]{1,0:T(8,128)S(1)} custom-call(f32[128,128]{1,0:T(8,128)S(1)} %cholesky.118), custom_call_target="Cholesky" | custom-call | tf_op jit(solution)/shard_map/jit(cholesky)/cholesky | solution.py:56
  110.2 2.5 %dynamic-slice_add_fusion = f32[896,256]{1,0:T(8,128)} fusion(f32[896,256]{1,0:T(8,128)} %collective-permute-done, f32[1792,256]{1,0:T(8,128)} %copy-done.1, s32[]{:T(128)S(6)} %select_n.32), kind=kLoop, calls=%fused_computation.17 | loop fusion | flops 229376 | bytes 2752516 | tf_op jit(solution)/shard_map/add | solution.py:36
  112.7 3.8 %all-to-all-start.4 = ((f32[16,56,256]{2,1,0:T(8,128)}), f32[16,56,256]{2,1,0:T(8,128)S(1)}, u32[]{:S(2)}, u32[]{:S(2)}) async-start(f32[16,56,256]{2,1,0:T(8,128)} %bitcast.59), calls=%async_computation.4 | async-start | bytes 1835008 | tf_op jit(solution)/shard_map/all_to_all | solution.py:14
  116.5 1.5 select_reduce_fusion.1
  118.0 11.3 %custom-call.14 = f32[1,128,128]{1,2,0:T(8,128)} custom-call(f32[1,128,128]{2,1,0:T(8,128)} %get-tuple-element.26), custom_call_target="InvertDiagBlocksLowerTriangular" | custom-call | tf_op jit(solution)/shard_map/jit(cholesky)/cholesky | solution.py:56
  129.3 1.0 constant_dynamic-update-slice_fusion
  130.3 0.9 convolution_subtract_fusion.1
  131.2 12.5 %cholesky.105 = f32[128,128]{1,0:T(8,128)S(1)} custom-call(f32[128,128]{1,0:T(8,128)} %convolution_subtract_fusion.1), custom_call_target="Cholesky" | custom-call | tf_op jit(solution)/shard_map/jit(cholesky)/cholesky | solution.py:56
  146.0 1.0 broadcast_in_dim.9
  147.0 6.4 %all-to-all-start.5 = ((f32[16,56,256]{2,1,0:T(8,128)}), f32[16,56,256]{2,1,0:T(8,128)S(1)}, u32[]{:S(2)}, u32[]{:S(2)}) async-start(f32[16,56,256]{2,1,0:T(8,128)} %broadcast_in_dim.9), calls=%async_computation.5 | async-start | bytes 1835008 | tf_op jit(solution)/shard_map/all_to_all | solution.py:20
  153.5 5.3 %while.1 = (s32[]{:T(128)}, f32[256,256]{1,0:T(8,128)S(1)}, s32[2,2]{1,0:T(2,128)S(1)}, f32[2,128,128]{2,1,0:T(8,128)}, s32[]{:T(128)}) while((s32[]{:T(128)}, f32[256,256]{1,0:T(8,128)S(1)}, s32[2,2]{1,0:T(2,128)S(1)}, f32[2,128,128]{2,1,0:T(8,128)}, s32[]{:T(128)}) %tuple.29), condition=%wide.while_cond, body=%wide.while_body.sunk | while | flops 2 | bytes 132705 | solution.py:57
  154.1 2.1 bitcast_dynamic-update-slice_fusion.2
  156.8 2.1 bitcast_dynamic-update-slice_fusion.2
  158.8 20.5 %custom-call.15 = f32[2,128,128]{1,2,0:T(8,128)S(1)} custom-call(f32[2,128,128]{2,1,0:T(8,128)} %get-tuple-element.10), custom_call_target="InvertDiagBlocksLowerTriangular" | custom-call | tf_op jit(solution)/shard_map/triangular_solve | solution.py:57
  179.3 2.9 %collective-permute-start.1 = (f32[896,256]{1,0:T(8,128)S(1)}, f32[896,256]{1,0:T(8,128)S(1)}, u32[]{:S(2)}, u32[]{:S(2)}) collective-permute-start(f32[896,256]{1,0:T(8,128)S(1)} %bitcast.60), channel_id=1, source_target_pairs={{0,16},{16,0},{32,48},{48,32},{64,80},{80,64},{96,112},{112,96},{1... | collective-permute-start | bytes 2752520 | tf_op jit(solution)/shard_map/ppermute | solution.py:39
  182.2 1.0 fusion.15
  183.2 1.0 convolution_subtract_fusion
  185.1 2.9 %multiply_reduce_fusion = (f32[256]{0:T(256)S(1)}, f32[1792,256]{1,0:T(8,128)}) fusion(f32[128,256]{1,0:T(8,128)S(1)} %fusion.18, f32[128,256]{1,0:T(8,128)S(1)} %fusion.15, f32[896,256]{1,0:T(8,128)S(1)} %get-tuple-element.22, f32[896,256]{1,0:T(8,128)S(1)} %get-tuple-element.21), kind=kOutput, calls=%fused_computation.12 | convolution fusion | flops 1410727680 | bytes 3933184 | tf_op jit(solution)/shard_map/dot_general | solution.py:59
  188.6 5.4 %all-to-all-start.6 = ((f32[16,1,256]{2,1,0:T(1,128)}), f32[16,1,256]{2,1,0:T(1,128)S(1)}, u32[]{:S(2)}, u32[]{:S(2)}) async-start(f32[16,1,256]{2,1,0:T(1,128)} %reshape.66), calls=%async_computation.6 | async-start | bytes 32768 | tf_op jit(solution)/shard_map/all_to_all | solution.py:20
  194.1 2.9 %fusion.1 = bf16[256,1792]{1,0:T(8,128)(2,1)} fusion(bf16[256,1792]{1,0:T(8,128)(2,1)S(1)} %add_convert_fusion, f32[1792,256]{1,0:T(8,128)} %get-tuple-element.30, f32[256,256]{1,0:T(8,128)S(1)} %fusion.11), kind=kOutput, calls=%fused_computation.6 | convolution fusion | flops 237240320 | bytes 3932160 | tf_op jit(solution)/shard_map/dot_general | solution.py:65
  196.9 8.5 %all-to-all-done.6 = f32[16,1,256]{2,1,0:T(1,128)S(1)} async-done(((f32[16,1,256]{2,1,0:T(1,128)}), f32[16,1,256]{2,1,0:T(1,128)S(1)}, u32[]{:S(2)}, u32[]{:S(2)}) %all-to-all-start.6) | async-done | bytes 16416 | tf_op jit(solution)/shard_map/all_to_all | solution.py:20
  205.5 2.6 %multiply_convert_fusion = bf16[1792,256]{1,0:T(8,128)(2,1)} fusion(f32[1792,256]{1,0:T(8,128)} %get-tuple-element.30, f32[256]{0:T(256)S(1)} %add_rsqrt_fusion), kind=kLoop, calls=%fused_computation.11 | loop fusion | flops 917504 | bytes 2753536 | tf_op jit(solution)/shard_map/convert_element_type | solution.py:63
  (43 shorter events, 8.3 us)
Async XLA Ops:
  0.6 1.8 copy-start
  32.3 24.0 %all-to-all-start.1 = ((f32[16,16,256]{2,1,0:T(8,128)}), f32[16,16,256]{2,1,0:T(8,128)S(1)}, u32[]{:S(2)}, u32[]{:S(2)}) async-start(f32[16,16,256]{2,1,0:T(8,128)} %broadcast_in_dim.7), calls=%async_computation.1 | async-start | bytes 524288 | tf_op jit(solution)/shard_map/all_to_all | solution.py:20
  57.7 1.3 copy-start.1
  59.9 50.3 %collective-permute-start = (f32[896,256]{1,0:T(8,128)}, f32[896,256]{1,0:T(8,128)}, u32[]{:S(2)}, u32[]{:S(2)}) collective-permute-start(f32[896,256]{1,0:T(8,128)} %constant_dynamic-slice_fusion.1), channel_id=1, source_target_pairs={{0,16},{16,0},{32,48},{48,32},{64,80},{80,64},{96,112},{112,96},{1... | collective-permute-start | bytes 2752520 | tf_op jit(solution)/shard_map/ppermute | solution.py:36
  85.4 12.8 %all-to-all-start.3 = ((f32[32,8,256]{2,1,0:T(8,128)}), f32[32,8,256]{2,1,0:T(8,128)S(1)}, u32[]{:S(2)}, u32[]{:S(2)}) async-start(f32[32,8,256]{2,1,0:T(8,128)} %broadcast_in_dim.8), calls=%async_computation.3 | async-start | bytes 524288 | tf_op jit(solution)/shard_map/all_to_all | solution.py:20
  110.2 2.6 %copy-start.3 = (f32[128,128]{1,0:T(8,128)}, f32[128,128]{1,0:T(8,128)S(1)}, u32[]{:S(2)}) copy-start(f32[128,128]{1,0:T(8,128)S(1)} %cholesky.50) | copy-start | bytes 196612
  112.7 33.2 %all-to-all-start.4 = ((f32[16,56,256]{2,1,0:T(8,128)}), f32[16,56,256]{2,1,0:T(8,128)S(1)}, u32[]{:S(2)}, u32[]{:S(2)}) async-start(f32[16,56,256]{2,1,0:T(8,128)} %bitcast.59), calls=%async_computation.4 | async-start | bytes 1835008 | tf_op jit(solution)/shard_map/all_to_all | solution.py:14
  147.0 32.4 %all-to-all-start.5 = ((f32[16,56,256]{2,1,0:T(8,128)}), f32[16,56,256]{2,1,0:T(8,128)S(1)}, u32[]{:S(2)}, u32[]{:S(2)}) async-start(f32[16,56,256]{2,1,0:T(8,128)} %broadcast_in_dim.9), calls=%async_computation.5 | async-start | bytes 1835008 | tf_op jit(solution)/shard_map/all_to_all | solution.py:20
  179.3 5.7 %collective-permute-start.1 = (f32[896,256]{1,0:T(8,128)S(1)}, f32[896,256]{1,0:T(8,128)S(1)}, u32[]{:S(2)}, u32[]{:S(2)}) collective-permute-start(f32[896,256]{1,0:T(8,128)S(1)} %bitcast.60), channel_id=1, source_target_pairs={{0,16},{16,0},{32,48},{48,32},{64,80},{80,64},{96,112},{112,96},{1... | collective-permute-start | bytes 2752520 | tf_op jit(solution)/shard_map/ppermute | solution.py:39
  185.0 9.1 %copy-start.2 = (f32[256,256]{1,0:T(8,128)}, f32[256,256]{1,0:T(8,128)S(1)}, u32[]{:S(2)}) copy-start(f32[256,256]{1,0:T(8,128)S(1)} %fusion.11) | copy-start | bytes 786436
  188.6 16.8 %all-to-all-start.6 = ((f32[16,1,256]{2,1,0:T(1,128)}), f32[16,1,256]{2,1,0:T(1,128)S(1)}, u32[]{:S(2)}, u32[]{:S(2)}) async-start(f32[16,1,256]{2,1,0:T(1,128)} %reshape.66), calls=%async_computation.6 | async-start | bytes 32768 | tf_op jit(solution)/shard_map/all_to_all | solution.py:20

commit v2 on v0

v2 whole, which is shorter than its diff:
```python
import functools
import jax
import jax.numpy as jnp
from jax import lax
from jax.experimental import pallas as pl
from jax.experimental.pallas import tpu as pltpu
from jax.sharding import Mesh, PartitionSpec as P

HIGHEST = lax.Precision.HIGHEST
VMEM = pl.BlockSpec(memory_space=pltpu.VMEM)


def scatter_sum(x, axis, count):
    moved = lax.all_to_all(x, axis, 0, 0, tiled=True)
    return jnp.sum(moved.reshape(count, x.shape[0] // count, x.shape[1]), axis=0)


def gather(x, axis, count):
    copies = jnp.broadcast_to(x[None], (count,) + x.shape).reshape(count * x.shape[0], x.shape[1])
    return lax.all_to_all(copies, axis, 0, 0, tiled=True)


def nt(a, b):
    return lax.dot_general(a, b, (((1,), (1,)), ((), ())), precision=HIGHEST, preferred_element_type=jnp.float32)

def factor_block(block):
    size = block.shape[0]
    rest = block
    done = []
    for start in range(0, size, 8):
        height = size - start
        row = lax.broadcasted_iota(jnp.int32, (height, 128), 0)
        cols = [jnp.broadcast_to(rest[:, start + m:start + m + 1], (height, 128)) for m in range(8)]
        tile = rest[:8]
        pivots = jnp.ones((8, 128), jnp.float32)
        gains = []
        for m in range(8):
            pivot = cols[m][m:m + 1]
            gain = jnp.where(row > m, cols[m] * (1.0 / pivot), 0.0)
            for q in range(m + 1, 8):
                cols[q] = cols[q] - gain * cols[q][m:m + 1]
            tile = tile - gain[:8] * tile[m:m + 1]
            pivots = jnp.where(row[:8] == m, pivot, pivots)
            gains.append(gain)
        done.append(tile * lax.rsqrt(pivots))
        if height > 8:
            rest = rest[8:]
            for m in range(8):
                rest = rest - gains[m][8:] * tile[m:m + 1]
    return jnp.concatenate(done, axis=0)

def inverse_factor_kernel(size, core_ref, mine_ref, other_ref, out_ref, a_ref, y_ref):
    n = out_ref.shape[0]
    first = core_ref[0] == 0
    mine = mine_ref[...].reshape(n // 2, n)
    other = other_ref[...].reshape(n // 2, n)
    a_ref[:n // 2, :] = jnp.where(first, mine, other)
    a_ref[n // 2:, :] = jnp.where(first, other, mine)
    r = lax.broadcasted_iota(jnp.int32, (n, n), 0)
    c = lax.broadcasted_iota(jnp.int32, (n, n), 1)
    y_ref[...] = jnp.where(r == c, 1.0, 0.0)
    r = lax.broadcasted_iota(jnp.int32, (size, 128), 0)
    c = lax.broadcasted_iota(jnp.int32, (size, 128), 1)
    for o in range(0, n, size):
        end = o + size
        base = o // 128 * 128
        diag = a_ref[o:end, base:base + 128]
        if o % 128:
            diag = pltpu.roll(diag, 128 - o % 128, 1)
        block = jnp.where(c < size, diag, jnp.where(c - size == r, 1.0, 0.0))
        small = factor_block(block)
        inverse = small[:, size:2 * size]
        value = jnp.dot(inverse, y_ref[o:end, :], precision=HIGHEST, preferred_element_type=jnp.float32)
        out_ref[o:end, :] = value
        if end < n:
            panel = nt(a_ref[end:, o:end], inverse)
            a_ref[end:, :] = a_ref[end:, :] - jnp.concatenate([jnp.zeros((n - end, end), jnp.float32), nt(panel, panel)], axis=1)
            y_ref[end:, :] = y_ref[end:, :] - jnp.dot(panel, value, precision=HIGHEST, preferred_element_type=jnp.float32)

def inverse_factor(core, mine, other, size=64):
    pieces, height, n = mine.shape
    small = n // 2 // pieces
    spec = pl.BlockSpec((pieces, small, n), lambda step: (0, height // small - 1, 0))
    return pl.pallas_call(
        functools.partial(inverse_factor_kernel, size),
        grid=(1,),
        out_shape=jax.ShapeDtypeStruct((n, n), jnp.float32),
        in_specs=[pl.BlockSpec(memory_space=pltpu.SMEM), spec, spec],
        out_specs=pl.BlockSpec((n, n), lambda step: (0, 0)),
        scratch_shapes=[pltpu.VMEM((n, n), jnp.float32), pltpu.VMEM((n, n), jnp.float32)],
        name="inverse_factor",
    )(core, mine, other)


def sum_copies_kernel(in_ref, out_ref):
    count = in_ref.shape[0]
    total = in_ref[0]
    for index in range(1, count):
        total = total + in_ref[index]
    for index in range(count):
        out_ref[index] = total


def sum_copies(parts):
    return pl.pallas_call(
        sum_copies_kernel,
        out_shape=jax.ShapeDtypeStruct(parts.shape, parts.dtype),
        in_specs=[VMEM],
        out_specs=VMEM,
        name="sum_copies",
    )(parts)


def right_kernel(core_ref, mine_ref, other_ref, inverse_ref, right_ref, sums_ref):
    chips, height, rank = mine_ref.shape
    swap = core_ref[0] != pl.program_id(0)
    rows = jnp.where(swap, other_ref[...], mine_ref[...]).reshape(chips * height, rank)
    right = nt(rows, inverse_ref[...])
    right_ref[...] = right
    sums = jnp.sum(right * right, axis=0, keepdims=True)

    @pl.when((pl.program_id(0) == 0) & (pl.program_id(1) == 0))
    def _():
        sums_ref[...] = sums

    @pl.when((pl.program_id(0) != 0) | (pl.program_id(1) != 0))
    def _():
        sums_ref[...] += sums


def right_and_sums(core, mine, other, inverse, steps=2):
    pieces, height, rank = mine.shape
    large = height - rank // 2 // pieces
    chips = pieces // steps
    spec = pl.BlockSpec((chips, large, rank), lambda half, step: (step, 0, 0))
    return pl.pallas_call(
        right_kernel,
        grid=(2, steps),
        out_shape=(
            jax.ShapeDtypeStruct((2 * pieces * large, rank), jnp.float32),
            jax.ShapeDtypeStruct((1, rank), jnp.float32),
        ),
        in_specs=[
            pl.BlockSpec(memory_space=pltpu.SMEM), spec, spec,
            pl.BlockSpec((rank, rank), lambda half, step: (0, 0)),
        ],
        out_specs=(
            pl.BlockSpec((chips * large, rank), lambda half, step: (half * steps + step, 0)),
            pl.BlockSpec((1, rank), lambda half, step: (0, 0)),
        ),
        name="right_and_sums",
    )(core, mine, other, inverse)


def feedback_kernel(left_ref, inverse_ref, right_ref, blend_ref, momentum_ref, factor_ref):
    factor = nt(left_ref[...], inverse_ref[...])
    factor_ref[...] = factor
    ortho = factor.astype(jnp.bfloat16)
    width = blend_ref.shape[1]
    tile = width // 2
    for at in range(0, width, tile):
        correction = lax.dot_general(
            ortho, right_ref[at:at + tile, :].astype(jnp.bfloat16), (((1,), (1,)), ((), ())),
            preferred_element_type=jnp.float32,
        )
        blend = blend_ref[:, at:at + tile].astype(jnp.float32)
        momentum_ref[:, at:at + tile] = (blend - 0.1 * correction).astype(jnp.bfloat16)


def feedback(left, inverse, right, blend):
    return pl.pallas_call(
        feedback_kernel,
        out_shape=(jax.ShapeDtypeStruct(blend.shape, blend.dtype), jax.ShapeDtypeStruct(left.shape, jnp.float32)),
        in_specs=[VMEM] * 4,
        out_specs=(VMEM, VMEM),
        compiler_params=pltpu.CompilerParams(vmem_limit_bytes=32 * 1024 * 1024),
        name="feedback",
    )(left, inverse, right, blend)


def products_kernel(pieces, left_ref, blend_ref, out_ref):
    left = left_ref[...]
    rank = left.shape[1]
    gram = lax.dot_general(left, left, (((0,), (0,)), ((), ())), precision=HIGHEST, preferred_element_type=jnp.float32)
    first = left.astype(jnp.bfloat16)
    rest = left - first.astype(jnp.float32)
    second = rest.astype(jnp.bfloat16)
    third = (rest - second.astype(jnp.float32)).astype(jnp.bfloat16)
    terms = jnp.concatenate([first, second, third], axis=1)
    wide = blend_ref.shape[1]
    large, small = wide // pieces, rank // pieces
    piece = large + small
    for part in range(2):
        half = wide // 2
        both = lax.dot_general(
            blend_ref[:, part * half:(part + 1) * half], terms, (((0,), (0,)), ((), ())),
            preferred_element_type=jnp.float32,
        )
        product = both[:, :rank] + both[:, rank:2 * rank] + both[:, 2 * rank:]
        for index in range(pieces // 2):
            at = (part * (pieces // 2) + index) * piece
            out_ref[at:at + large, :] = product[index * large:(index + 1) * large]
    for index in range(pieces):
        at = index * piece + large
        out_ref[at:at + small, :] = gram[index * small:(index + 1) * small]


def products(left, blend, pieces):
    return pl.pallas_call(
        functools.partial(products_kernel, pieces),
        out_shape=jax.ShapeDtypeStruct((blend.shape[1] + left.shape[1], left.shape[1]), jnp.float32),
        in_specs=[VMEM, VMEM],
        out_specs=VMEM,
        compiler_params=pltpu.CompilerParams(vmem_limit_bytes=32 * 1024 * 1024),
        name="products",
    )(left, blend)


def local(chips, cores, cols, momentum, gradient, right_factor):
    blend = (momentum.astype(jnp.float32) + gradient.astype(jnp.float32)).astype(jnp.bfloat16)
    left = jnp.dot(blend, right_factor, preferred_element_type=jnp.float32)
    left = gather(scatter_sum(left, "col", cols), "col", cols)

    both = products(left, blend, chips * cores)
    both = scatter_sum(both, "core", cores)
    both = lax.all_to_all(both.reshape(chips, -1, both.shape[1]), "chip", 0, 0)
    mine = lax.all_to_all(sum_copies(both), "chip", 0, 0)
    other = lax.ppermute(mine, "core", [(0, 1), (1, 0)])
    core = lax.axis_index("core").astype(jnp.int32).reshape(1)
    inverse = inverse_factor(core, mine, other)
    right, sums = right_and_sums(core, mine, other, inverse)
    total = jnp.sum(gather(sums, "col", cols), axis=0)
    new_momentum, left_factor = feedback(left, inverse, right, blend)
    new_right = (right * lax.rsqrt(total + 1e-08)).astype(jnp.bfloat16)
    return (new_momentum, new_right, left_factor)


def solution(mesh):
    rows, cols = mesh.devices.shape
    chips, cores = rows // 2, 2
    split = Mesh(mesh.devices.reshape(chips, cores, cols), ("chip", "core", "col"))
    row = ("chip", "core")
    placed = (P(row, "col"), P(row, "col"), P("col", None))
    return jax.shard_map(
        functools.partial(local, chips, cores, cols),
        mesh=split,
        in_specs=placed,
        out_specs=(P(row, "col"), P("col", None), P(row, None)),
        check_vma=False,
    )
```

time: 536 us -> 160 us (0.30); the launches traced: 528 us -> 159 us
  waiting for transfers between devices: 407 us -> 10.2 us
  blocking collectives: 24.3 us -> 106 us
  other arithmetic: 59.5 us -> 6.23 us
  Pallas kernels: 0 us -> 22.3 us
  between operations: 15.2 us -> 0.72 us
  matrix products: 12.7 us -> 0.41 us
  starting transfers between devices: 0.12 us -> 10.4 us
  local copies, waits for them, and re-layouts: 9.02 us -> 2.82 us
    psum x3 -> x0, waiting for transfers between devices: 407 us -> none  [the longest x1 140 us: local(): lax.psum(jnp.dot(left.T, left, precision=lax.Precision.HIGHEST), 'row')]
    all_to_all x0 -> x5, blocking collectives: none -> 106 us  [the longest x2 41 us: scatter_sum(): moved = lax.all_to_all(x, axis, 0, 0, tiled=True)]
    another operation x10 -> x0, other arithmetic: 55.5 us -> none  [the longest x6 34 us: local(): lower = jnp.linalg.cholesky(gram)]
    psum x1 -> x0, blocking collectives: 24.3 us -> none  [local(): total = lax.psum(jnp.sum(right * right, axis=0), 'col')]
    pallas_call x0 -> x5, Pallas kernels: none -> 22.3 us  [the longest x1 11.4 us: inverse_factor(): pl.pallas_call(functools.partial(inverse_factor_kernel, size), grid=(1,),...]
    dot_general x4 -> x1, matrix products: 9.49 us -> 0.41 us  [local(): left = jnp.dot(blend, right_factor, preferred_element_type=jnp.float32)]
    all_to_all x0 -> x1, waiting for transfers between devices: none -> 7.81 us  [gather(): return lax.all_to_all(copies, axis, 0, 0, tiled=True)]
    all_to_all x0 -> x1, starting transfers between devices: none -> 5.41 us  [gather(): return lax.all_to_all(copies, axis, 0, 0, tiled=True)]
  transfers between devices with their start and end apart: 3 -> 2, of which waited for: 3 -> 2; matrix products, arithmetic and copies ran while one was open for 0% -> 0% of each run, Pallas kernels for 0% -> 1%
where the time goes in v2:
time: 160 us; the launch traced here: 159 us
  blocking collectives  106 us (66%)
  Pallas kernels  22.3 us (14%)
  starting transfers between devices  10.4 us (6%)
  waiting for transfers between devices  10.2 us (6%)
  other arithmetic  6.23 us (4%)
  local copies, waits for them, and re-layouts  2.82 us (2%)
    all_to_all x2, blocking collectives, scatter_sum(): moved = lax.all_to_all(x, axis, 0, 0, tiled=True)  41 us
    all_to_all x1, blocking collectives, gather(): return lax.all_to_all(copies, axis, 0, 0, tiled=True)  23.8 us
    all_to_all x1, blocking collectives, local(): both = lax.all_to_all(both.reshape(chips, -1, both.shape[1]), 'chip', 0, 0)  22.6 us
    all_to_all x1, blocking collectives, local(): mine = lax.all_to_all(sum_copies(both), 'chip', 0, 0)  18.7 us
    pallas_call x1, Pallas kernels, inverse_factor(): pl.pallas_call(functools.partial(inverse_factor_kernel, size), grid=(1,),...  11.4 us
    all_to_all x1, waiting for transfers between devices, gather(): return lax.all_to_all(copies, axis, 0, 0, tiled=True)  7.81 us
    all_to_all x1, starting transfers between devices, gather(): return lax.all_to_all(copies, axis, 0, 0, tiled=True)  5.41 us
    pallas_call x1, Pallas kernels, right_and_sums(): pl.pallas_call(right_kernel, grid=(2, steps), out_shape=(jax.ShapeDtypeSt...  5.27 us
  transfers between devices with their start and end apart: 2, of which 2 were waited for; matrix products, arithmetic and copies ran while one was open for 0% of the time, Pallas kernels for 1%

profile of v2, /device:TPU:1, one launch (start us, length us, event | category | flops | bytes accessed | tf_op | source)
XLA Modules:
  0.0 159.2 jit_solution(2820089428463816373)
XLA Ops:
  0.6 0.0 copy-start
  0.6 1.7 %add_convert_fusion.blend_ref = bf16[256,1792]{1,0:T(8,128)(2,1)S(1)} fusion(bf16[256,1792]{1,0:T(8,128)(2,1)} %param.4, bf16[256,1792]{1,0:T(8,128)(2,1)} %param.3), kind=kLoop, calls=%fused_computation.1 | loop fusion | flops 1835008 | bytes 2752512 | tf_op jit(solution)/shard_map/convert_element_type | solution.py:220
  2.4 0.0 copy-done
  2.4 0.4 fusion
  2.8 28.7 %all_to_all.42 = f32[16,16,256]{2,1,0:T(8,128)S(1)} all-to-all(f32[16,16,256]{2,1,0:T(8,128)S(1)} %bitcast.12), channel_id=1, replica_groups=mesh['chip'=16,'core'=2,'col'=16] {'col'}, dimensions={0} | all-to-all | bytes 524288 | tf_op jit(solution)/shard_map/all_to_all | solution.py:14
  31.6 23.8 %all_to_all.43 = f32[16,16,256]{2,1,0:T(8,128)S(1)} all-to-all(f32[16,16,256]{2,1,0:T(8,128)S(1)} %broadcast_in_dim.2), channel_id=1, replica_groups=mesh['chip'=16,'core'=2,'col'=16] {'col'}, dimensions={0} | all-to-all | bytes 524288 | tf_op jit(solution)/shard_map/all_to_all | solution.py:20
  55.4 1.2 products.1
  56.6 12.3 %all_to_all.44 = f32[2,1024,256]{2,1,0:T(8,128)} all-to-all(f32[2,1024,256]{2,1,0:T(8,128)S(1)} %bitcast.8), channel_id=1, replica_groups=mesh['chip'=16,'core'=2,'col'=16] {'core'}, dimensions={0} | all-to-all | bytes 4194304 | tf_op jit(solution)/shard_map/all_to_all | solution.py:14
  68.8 1.8 %reduce_sum.28 = f32[1024,256]{1,0:T(8,128)S(1)} reduce(f32[2,1024,256]{2,1,0:T(8,128)} %all_to_all.44, f32[]{:T(128)} %constant.2.clone.1), dimensions={0}, to_apply=%region_1.0 | reduce | flops 262144 | bytes 3145732 | tf_op jit(solution)/shard_map/reduce_sum | solution.py:15
  70.7 22.6 %all_to_all.45.in_ref = f32[16,64,256]{2,1,0:T(8,128)} all-to-all(f32[16,64,256]{2,1,0:T(8,128)S(1)} %bitcast.11), channel_id=1, replica_groups=mesh['chip'=16,'core'=2,'col'=16] {'chip'}, dimensions={0} | all-to-all | bytes 2097152 | tf_op jit(solution)/shard_map/all_to_all | solution.py:226
  93.3 2.4 %sum_copies.1 = f32[16,64,256]{2,1,0:T(8,128)} custom-call(f32[16,64,256]{2,1,0:T(8,128)} %all_to_all.45.in_ref), custom_call_target="tpu_custom_call" | custom-call | tf_op jit(solution)/shard_map/sum_copies/pallas_call | solution.py:105
  95.7 18.7 %all_to_all.46.mine_ref = f32[16,64,256]{2,1,0:T(8,128)S(1)} all-to-all(f32[16,64,256]{2,1,0:T(8,128)} %sum_copies.1), channel_id=1, replica_groups=mesh['chip'=16,'core'=2,'col'=16] {'chip'}, dimensions={0} | all-to-all | bytes 2097152 | tf_op jit(solution)/shard_map/all_to_all | solution.py:227
  114.4 0.0 copy-start.3
  114.4 5.0 %collective-permute-start = (f32[16,64,256]{2,1,0:T(8,128)S(1)}, f32[16,64,256]{2,1,0:T(8,128)}, u32[]{:S(2)}, u32[]{:S(2)}) collective-permute-start(f32[16,64,256]{2,1,0:T(8,128)S(1)} %all_to_all.46.mine_ref), channel_id=1, source_target_pairs={{0,16},{16,0},{1,17},{17,1},{2,18},{18,2},{3,19},{19,3},{4,20},{20... | collective-permute-start | bytes 3145736 | tf_op jit(solution)/shard_map/ppermute | solution.py:228
  119.4 2.4 %collective-permute-done.other_ref = f32[16,64,256]{2,1,0:T(8,128)} collective-permute-done((f32[16,64,256]{2,1,0:T(8,128)S(1)}, f32[16,64,256]{2,1,0:T(8,128)}, u32[]{:S(2)}, u32[]{:S(2)}) %collective-permute-start) | collective-permute-done | bytes 1048608 | tf_op jit(solution)/shard_map/ppermute | solution.py:228
  121.8 0.0 copy-done.3
  121.8 11.4 %inverse_factor.1.inverse_ref = f32[256,256]{1,0:T(8,128)} custom-call(s32[1]{0:T(128)} %bitcast.2.core_ref, f32[16,64,256]{2,1,0:T(8,128)} %copy-done.3, f32[16,64,256]{2,1,0:T(8,128)} %collective-permute-done.other_ref), custom_call_target="tpu_custom_call" | custom-call | tf_op jit(solution)/shard_map/inverse_factor/pallas_call | solution.py:84
  133.3 0.0 copy-start.2
  133.3 5.3 %right_and_sums.1 = (f32[1792,256]{1,0:T(8,128)}, f32[1,256]{1,0:T(1,128)}) custom-call(s32[1]{0:T(128)} %bitcast.2.core_ref, f32[16,64,256]{2,1,0:T(8,128)} %copy-done.3, f32[16,64,256]{2,1,0:T(8,128)} %collective-permute-done.other_ref, f32[256,256]{1,0:T(8,128)} %inverse_factor.1.inverse_ref), custom_call_target="tpu_custom_call" | custom-call | tf_op jit(solution)/shard_map/right_and_sums/pallas_call | solution.py:136
  138.5 1.3 reshape.43
  139.8 5.4 %all-to-all-start.5 = ((f32[16,1,256]{2,1,0:T(1,128)}), f32[16,1,256]{2,1,0:T(1,128)S(1)}, u32[]{:S(2)}, u32[]{:S(2)}) async-start(f32[16,1,256]{2,1,0:T(1,128)} %reshape.43), calls=%async_computation.5 | async-start | bytes 32768 | tf_op jit(solution)/shard_map/all_to_all | solution.py:20
  145.2 0.0 copy-done.2
  145.3 0.0 copy-start.1
  145.3 1.5 copy-done.1
  146.8 2.1 %feedback.1 = (bf16[256,1792]{1,0:T(8,128)(2,1)}, f32[256,256]{1,0:T(8,128)}) custom-call(f32[256,256]{1,0:T(8,128)S(1)} %bitcast.10, f32[256,256]{1,0:T(8,128)S(1)} %copy-done.2, f32[1792,256]{1,0:T(8,128)S(1)} %copy-done.1, bf16[256,1792]{1,0:T(8,128)(2,1)S(1)} %add_convert_fusion.blend_ref), custom_call_target="tpu_custom_call" | custom-call | tf_op jit(solution)/shard_map/feedback/pallas_call | solution.py:171
  148.8 7.8 %all-to-all-done.5 = f32[16,1,256]{2,1,0:T(1,128)S(1)} async-done(((f32[16,1,256]{2,1,0:T(1,128)}), f32[16,1,256]{2,1,0:T(1,128)S(1)}, u32[]{:S(2)}, u32[]{:S(2)}) %all-to-all-start.5) | async-done | bytes 16416 | tf_op jit(solution)/shard_map/all_to_all | solution.py:20
  156.7 2.6 %multiply_convert_fusion = bf16[1792,256]{1,0:T(8,128)(2,1)} fusion(f32[1792,256]{1,0:T(8,128)} %get-tuple-element.7.right_ref, f32[256]{0:T(256)S(1)} %add_rsqrt_fusion), kind=kLoop, calls=%fused_computation | loop fusion | flops 917504 | bytes 2753536 | tf_op jit(solution)/shard_map/convert_element_type | solution.py:234
  (4 shorter events, 0.1 us)
Async XLA Ops:
  0.6 1.8 %copy-start = (bf16[1792,256]{1,0:T(8,128)(2,1)S(1)}, bf16[1792,256]{1,0:T(8,128)(2,1)}, u32[]{:S(2)}) copy-start(bf16[1792,256]{1,0:T(8,128)(2,1)} %param.5) | copy-start | bytes 2752516
  114.4 7.4 %copy-start.3 = (f32[16,64,256]{2,1,0:T(8,128)}, f32[16,64,256]{2,1,0:T(8,128)S(1)}, u32[]{:S(2)}) copy-start(f32[16,64,256]{2,1,0:T(8,128)S(1)} %all_to_all.46.mine_ref) | copy-start | bytes 3145732
  114.4 7.4 %collective-permute-start = (f32[16,64,256]{2,1,0:T(8,128)S(1)}, f32[16,64,256]{2,1,0:T(8,128)}, u32[]{:S(2)}, u32[]{:S(2)}) collective-permute-start(f32[16,64,256]{2,1,0:T(8,128)S(1)} %all_to_all.46.mine_ref), channel_id=1, source_target_pairs={{0,16},{16,0},{1,17},{17,1},{2,18},{18,2},{3,19},{19,3},{4,20},{20... | collective-permute-start | bytes 3145736 | tf_op jit(solution)/shard_map/ppermute | solution.py:228
  133.3 12.0 %copy-start.2 = (f32[256,256]{1,0:T(8,128)S(1)}, f32[256,256]{1,0:T(8,128)}, u32[]{:S(2)}) copy-start(f32[256,256]{1,0:T(8,128)} %inverse_factor.1.inverse_ref) | copy-start | bytes 786436
  139.8 16.8 %all-to-all-start.5 = ((f32[16,1,256]{2,1,0:T(1,128)}), f32[16,1,256]{2,1,0:T(1,128)S(1)}, u32[]{:S(2)}, u32[]{:S(2)}) async-start(f32[16,1,256]{2,1,0:T(1,128)} %reshape.43), calls=%async_computation.5 | async-start | bytes 32768 | tf_op jit(solution)/shard_map/all_to_all | solution.py:20
  145.3 1.5 copy-start.1

commit v3 on v2

v3 whole, which is shorter than its diff:
```python
import functools
import jax
import jax.numpy as jnp
from jax import lax
from jax.experimental import pallas as pl
from jax.experimental.pallas import tpu as pltpu
from jax.sharding import Mesh, PartitionSpec as P

HIGHEST = lax.Precision.HIGHEST
VMEM = pl.BlockSpec(memory_space=pltpu.VMEM)


def scatter_sum(x, axis, count):
    moved = lax.all_to_all(x, axis, 0, 0, tiled=True)
    return jnp.sum(moved.reshape(count, x.shape[0] // count, x.shape[1]), axis=0)


def gather(x, axis, count):
    copies = jnp.broadcast_to(x[None], (count,) + x.shape).reshape(count * x.shape[0], x.shape[1])
    return lax.all_to_all(copies, axis, 0, 0, tiled=True)


def nt(a, b):
    return lax.dot_general(a, b, (((1,), (1,)), ((), ())), precision=HIGHEST, preferred_element_type=jnp.float32)


def nn(a, b):
    return lax.dot_general(a, b, (((1,), (0,)), ((), ())), precision=HIGHEST, preferred_element_type=jnp.float32)


def factor_block(block, panel):
    size = block.shape[0]
    rest = block
    done = []
    for start in range(0, size, panel):
        height = size - start
        row = lax.broadcasted_iota(jnp.int32, (height, 128), 0)
        cols = [jnp.broadcast_to(rest[:, start + m:start + m + 1], (height, 128)) for m in range(panel)]
        tile = rest[:panel]
        pivots = jnp.ones((panel, 128), jnp.float32)
        gains = []
        for m in range(0, panel, 2):
            top = cols[m][m:m + 1]
            side = cols[m + 1][m:m + 1]
            low = cols[m + 1][m + 1:m + 2]
            det = top * low - side * side
            rtop = 1.0 / top
            rlow = top * (1.0 / det)
            slope = side * rtop
            g0 = jnp.where(row > m, cols[m] * rtop, 0.0)
            nxt = cols[m + 1] - g0 * side
            g1 = jnp.where(row > m + 1, nxt * rlow, 0.0)
            for q in range(m + 2, panel):
                u = cols[q][m:m + 1]
                v = cols[q][m + 1:m + 2] - slope * u
                cols[q] = (cols[q] - g0 * u) - g1 * v
            tile = tile - g0[:panel] * tile[m:m + 1]
            tile = tile - g1[:panel] * tile[m + 1:m + 2]
            pivots = jnp.where(row[:panel] == m, top, jnp.where(row[:panel] == m + 1, det * rtop, pivots))
            gains += [g0, g1]
        done.append(tile * lax.rsqrt(pivots))
        if height > panel:
            rest = rest[panel:]
            for m in range(panel):
                rest = rest - gains[m][panel:] * tile[m:m + 1]
    return jnp.concatenate(done, axis=0)


def inverse_factor_kernel(size, panel, mine_ref, out_ref, a_ref, y_ref):
    n = out_ref.shape[0]
    pieces, height, _ = mine_ref.shape
    r = lax.broadcasted_iota(jnp.int32, (n, n), 0)
    c = lax.broadcasted_iota(jnp.int32, (n, n), 1)
    gram = mine_ref[:, height - n // pieces:, :].reshape(n, n)
    diagonal = jnp.where(r == c, gram, 0.0)
    across = lax.rsqrt(jnp.sum(diagonal, axis=0, keepdims=True))
    down = lax.rsqrt(jnp.sum(diagonal, axis=1, keepdims=True))
    a_ref[...] = gram * across * down
    y_ref[...] = jnp.where(r == c, across, 0.0)
    count = n // size
    a = {}
    for i in range(count):
        for j in range(i + 1):
            a[i, j] = a_ref[i * size:(i + 1) * size, j * size:(j + 1) * size]
    eye = jnp.where(r[:size, :size] == c[:size, :size], 1.0, 0.0)
    y = [y_ref[i * size:(i + 1) * size, :] for i in range(count)]
    for k in range(count):
        small = factor_block(jnp.concatenate([a[k, k], eye], axis=1), panel)
        inverse = small[:, size:2 * size]
        p = {}
        for i in range(k + 1, count):
            p[i] = nt(a[i, k], inverse)
            for j in range(k + 1, i + 1):
                a[i, j] = a[i, j] - nt(p[i], p[j])
        lim = ((k + 1) * size + 127) // 128 * 128
        value = nn(inverse, y[k][:, :lim])
        out_ref[k * size:(k + 1) * size, :lim] = value
        if lim < n:
            out_ref[k * size:(k + 1) * size, lim:] = jnp.zeros((size, n - lim), jnp.float32)
        for i in range(k + 1, count):
            left = y[i][:, :lim] - nn(p[i], value)
            y[i] = left if lim == n else jnp.concatenate([left, y[i][:, lim:]], axis=1)


def inverse_factor(mine, size=64, panel=16):
    n = mine.shape[2]
    return pl.pallas_call(
        functools.partial(inverse_factor_kernel, size, panel),
        out_shape=jax.ShapeDtypeStruct((n, n), jnp.float32),
        in_specs=[VMEM],
        out_specs=VMEM,
        scratch_shapes=[pltpu.VMEM((n, n), jnp.float32), pltpu.VMEM((n, n), jnp.float32)],
        compiler_params=pltpu.CompilerParams(vmem_limit_bytes=8 * 1024 * 1024),
        name="inverse_factor",
    )(mine)


def sum_copies_kernel(in_ref, out_ref):
    count = in_ref.shape[0]
    total = in_ref[0]
    for index in range(1, count):
        total = total + in_ref[index]
    for index in range(count):
        out_ref[index] = total


def sum_copies(parts):
    return pl.pallas_call(
        sum_copies_kernel,
        out_shape=jax.ShapeDtypeStruct(parts.shape, parts.dtype),
        in_specs=[VMEM],
        out_specs=VMEM,
        compiler_params=pltpu.CompilerParams(vmem_limit_bytes=8 * 1024 * 1024),
        name="sum_copies",
    )(parts)


def right_kernel(mine_ref, inverse_ref, right_ref, sums_ref):
    pieces, height, rank = mine_ref.shape
    large = right_ref.shape[0] // pieces
    rows = mine_ref[:, :large, :].reshape(pieces * large, rank)
    right = nt(rows, inverse_ref[...])
    right_ref[...] = right
    sums_ref[...] = jnp.broadcast_to(jnp.sum(right * right, axis=0)[None, None], sums_ref.shape)


def right_and_sums(mine, inverse, count):
    pieces, height, rank = mine.shape
    large = height - rank // pieces
    return pl.pallas_call(
        right_kernel,
        out_shape=(
            jax.ShapeDtypeStruct((pieces * large, rank), jnp.float32),
            jax.ShapeDtypeStruct((count, 1, rank), jnp.float32),
        ),
        in_specs=[VMEM, VMEM],
        out_specs=(VMEM, VMEM),
        compiler_params=pltpu.CompilerParams(vmem_limit_bytes=10 * 1024 * 1024),
        name="right_and_sums",
    )(mine, inverse)


def sum_pair_kernel(in_ref, out_ref):
    out_ref[...] = in_ref[0] + in_ref[1]


def sum_pair(parts):
    return pl.pallas_call(
        sum_pair_kernel,
        out_shape=jax.ShapeDtypeStruct(parts.shape[1:], parts.dtype),
        in_specs=[VMEM],
        out_specs=VMEM,
        compiler_params=pltpu.CompilerParams(vmem_limit_bytes=8 * 1024 * 1024),
        name="sum_pair",
    )(parts)


def feedback_kernel(core_ref, left_ref, inverse_ref, mine_ref, other_ref, blend_ref, momentum_ref, factor_ref):
    factor = nt(left_ref[...], inverse_ref[...])
    factor_ref[...] = factor
    ortho = factor.astype(jnp.bfloat16)
    half = mine_ref.shape[0]
    for part in range(2):
        right = jnp.where(core_ref[0] == part, mine_ref[...], other_ref[...])
        correction = lax.dot_general(
            ortho, right.astype(jnp.bfloat16), (((1,), (1,)), ((), ())), preferred_element_type=jnp.float32
        )
        at = part * half
        blend = blend_ref[:, at:at + half].astype(jnp.float32)
        momentum_ref[:, at:at + half] = (blend - 0.1 * correction).astype(jnp.bfloat16)


def feedback(core, left, inverse, mine, other, blend):
    return pl.pallas_call(
        feedback_kernel,
        out_shape=(jax.ShapeDtypeStruct(blend.shape, blend.dtype), jax.ShapeDtypeStruct(left.shape, jnp.float32)),
        in_specs=[pl.BlockSpec(memory_space=pltpu.SMEM)] + [VMEM] * 5,
        out_specs=(VMEM, VMEM),
        compiler_params=pltpu.CompilerParams(vmem_limit_bytes=12 * 1024 * 1024),
        cost_estimate=pl.CostEstimate(flops=0, bytes_accessed=0, transcendentals=0),
        name="feedback",
    )(core, left, inverse, mine, other, blend)


def normalize_kernel(core_ref, mine_ref, other_ref, sums_ref, out_ref):
    scale = lax.rsqrt(jnp.sum(sums_ref[...], axis=0) + 1e-08)
    half = mine_ref.shape[0]
    for part in range(2):
        right = jnp.where(core_ref[0] == part, mine_ref[...], other_ref[...])
        out_ref[part * half:(part + 1) * half, :] = (right * scale).astype(jnp.bfloat16)


def normalize(core, mine, other, sums):
    rows, rank = mine.shape
    return pl.pallas_call(
        normalize_kernel,
        out_shape=jax.ShapeDtypeStruct((2 * rows, rank), jnp.bfloat16),
        in_specs=[pl.BlockSpec(memory_space=pltpu.SMEM)] + [VMEM] * 3,
        out_specs=VMEM,
        compiler_params=pltpu.CompilerParams(vmem_limit_bytes=8 * 1024 * 1024),
        name="normalize",
    )(core, mine, other, sums)


def products_kernel(left_ref, blend_ref, out_ref):
    left = left_ref[...]
    rank = left.shape[1]
    cores, chips = out_ref.shape[:2]
    gram = lax.dot_general(left, left, (((0,), (0,)), ((), ())), precision=HIGHEST, preferred_element_type=jnp.float32)
    first = left.astype(jnp.bfloat16)
    rest = left - first.astype(jnp.float32)
    second = rest.astype(jnp.bfloat16)
    third = (rest - second.astype(jnp.float32)).astype(jnp.bfloat16)
    terms = jnp.concatenate([first, second, third], axis=1)
    half = blend_ref.shape[1] // cores
    large, small = half // chips, rank // chips
    for core in range(cores):
        both = lax.dot_general(
            blend_ref[:, core * half:(core + 1) * half], terms, (((0,), (0,)), ((), ())),
            preferred_element_type=jnp.float32,
        )
        product = both[:, :rank] + both[:, rank:2 * rank] + both[:, 2 * rank:]
        for chip in range(chips):
            out_ref[core, chip, :large, :] = product[chip * large:(chip + 1) * large]
            out_ref[core, chip, large:, :] = gram[chip * small:(chip + 1) * small]


def products(left, blend, cores, chips):
    rank = left.shape[1]
    height = blend.shape[1] // cores // chips + rank // chips
    return pl.pallas_call(
        products_kernel,
        out_shape=jax.ShapeDtypeStruct((cores, chips, height, rank), jnp.float32),
        in_specs=[VMEM, VMEM],
        out_specs=VMEM,
        compiler_params=pltpu.CompilerParams(vmem_limit_bytes=12 * 1024 * 1024),
        name="products",
    )(left, blend)


def local(chips, cores, cols, momentum, gradient, right_factor):
    blend = (momentum.astype(jnp.float32) + gradient.astype(jnp.float32)).astype(jnp.bfloat16)
    left = jnp.dot(blend, right_factor, preferred_element_type=jnp.float32)
    left = gather(scatter_sum(left, "col", cols), "col", cols)

    both = sum_pair(lax.all_to_all(products(left, blend, cores, chips), "core", 0, 0))
    mine = lax.all_to_all(sum_copies(lax.all_to_all(both, "chip", 0, 0)), "chip", 0, 0)
    inverse = inverse_factor(mine)
    swap = [(0, 1), (1, 0)]
    core = lax.axis_index("core").astype(jnp.int32).reshape(1)
    right, sums = right_and_sums(mine, inverse, cores * cols)
    sums = lax.all_to_all(sums, ("core", "col"), 0, 0)
    other = lax.ppermute(right, "core", swap)
    new_momentum, left_factor = feedback(core, left, inverse, right, other, blend)
    new_right = normalize(core, right, other, sums)
    return (new_momentum, new_right, left_factor)


def solution(mesh):
    rows, cols = mesh.devices.shape
    chips, cores = rows // 2, 2
    split = Mesh(mesh.devices.reshape(chips, cores, cols), ("chip", "core", "col"))
    row = ("chip", "core")
    placed = (P(row, "col"), P(row, "col"), P("col", None))
    return jax.shard_map(
        functools.partial(local, chips, cores, cols),
        mesh=split,
        in_specs=placed,
        out_specs=(P(row, "col"), P("col", None), P(row, None)),
        check_vma=False,
    )
```

time: 160 us -> 148 us (0.925)
  Pallas kernels: 22.3 us -> 16.5 us
  other arithmetic: 6.23 us -> 1.77 us
  local copies, waits for them, and re-layouts: 2.82 us -> 0.03 us
  blocking collectives: 106 us -> 108 us
    all_to_all x2 -> x3, blocking collectives: 41.3 us -> 55.3 us  [the longest x1 24.1 us: local(): lax.all_to_all(both, 'chip', 0, 0)]
    all_to_all x2 -> x1, blocking collectives: 41 us -> 28.7 us  [scatter_sum(): moved = lax.all_to_all(x, axis, 0, 0, tiled=True)]
    pallas_call x3 -> x5, Pallas kernels: 17.9 us -> 13.1 us  [the longest x1 7.94 us: inverse_factor(): pl.pallas_call(functools.partial(inverse_factor_kernel, size, panel), out...]
    convert_element_type x1 -> x0, other arithmetic: 2.57 us -> none  [local(): new_right = (right * lax.rsqrt(total + 1e-08)).astype(jnp.bfloat16)]
    ppermute x1, waiting for transfers between devices: 2.39 us -> 0.01 us  [local(): other = lax.ppermute(right, 'core', swap)]
    pallas_call x1, Pallas kernels: 2.38 us -> 0.09 us  [sum_copies(): pl.pallas_call(sum_copies_kernel, out_shape=jax.ShapeDtypeStruct(parts.sh...]
    reduce_sum x2 -> x1, other arithmetic: 1.87 us -> 0.02 us  [scatter_sum(): jnp.sum(moved.reshape(count, x.shape[0] // count, x.shape[1]), axis=0)]
  transfers between devices with their start and end apart: 2 -> 2, of which waited for: 2 -> 1; matrix products, arithmetic and copies ran while one was open for 0% -> 0% of each run, Pallas kernels for 1% -> 2%
where the time goes in v3:
time: 148 us; the launch traced here: 147 us
  blocking collectives  108 us (73%)
  Pallas kernels  16.5 us (11%)
  starting transfers between devices  10.9 us (7%)
  waiting for transfers between devices  9.19 us (6%)
  other arithmetic  1.77 us (1%)
    all_to_all x1, blocking collectives, scatter_sum(): moved = lax.all_to_all(x, axis, 0, 0, tiled=True)  28.7 us
    all_to_all x1, blocking collectives, local(): lax.all_to_all(both, 'chip', 0, 0)  24.1 us
    all_to_all x1, blocking collectives, gather(): return lax.all_to_all(copies, axis, 0, 0, tiled=True)  23.8 us
    all_to_all x1, blocking collectives, local(): lax.all_to_all(sum_copies(lax.all_to_all(both, 'chip', 0, 0)), 'chip', 0, 0)  19.5 us
    all_to_all x1, blocking collectives, local(): lax.all_to_all(products(left, blend, cores, chips), 'core', 0, 0)  11.6 us
    all_to_all x1, waiting for transfers between devices, local(): sums = lax.all_to_all(sums, ('core', 'col'), 0, 0)  9.19 us
    pallas_call x1, Pallas kernels, inverse_factor(): pl.pallas_call(functools.partial(inverse_factor_kernel, size, panel), out...  7.94 us
    all_to_all x1, starting transfers between devices, local(): sums = lax.all_to_all(sums, ('core', 'col'), 0, 0)  5.88 us
  transfers between devices with their start and end apart: 2, of which 1 were waited for; matrix products, arithmetic and copies ran while one was open for 0% of the time, Pallas kernels for 2%

profile of v3, /device:TPU:1, one launch (start us, length us, event | category | flops | bytes accessed | tf_op | source)
XLA Modules:
  0.0 147.3 jit_solution(2069851570695468501)
XLA Ops:
  0.6 0.0 copy-start
  0.6 1.7 %add_convert_fusion.blend_ref = bf16[256,1792]{1,0:T(8,128)(2,1)S(1)} fusion(bf16[256,1792]{1,0:T(8,128)(2,1)} %param.4, bf16[256,1792]{1,0:T(8,128)(2,1)} %param.3), kind=kLoop, calls=%fused_computation | loop fusion | flops 1835008 | bytes 2752512 | tf_op jit(solution)/shard_map/convert_element_type | solution.py:262
  2.4 0.0 copy-done
  2.4 0.4 fusion
  2.8 28.7 %all_to_all.37 = f32[16,16,256]{2,1,0:T(8,128)S(1)} all-to-all(f32[16,16,256]{2,1,0:T(8,128)S(1)} %bitcast.7), channel_id=1, replica_groups=mesh['chip'=16,'core'=2,'col'=16] {'col'}, dimensions={0} | all-to-all | bytes 524288 | tf_op jit(solution)/shard_map/all_to_all | solution.py:14
  31.6 23.8 %all_to_all.38 = f32[16,16,256]{2,1,0:T(8,128)S(1)} all-to-all(f32[16,16,256]{2,1,0:T(8,128)S(1)} %broadcast_in_dim.2), channel_id=1, replica_groups=mesh['chip'=16,'core'=2,'col'=16] {'col'}, dimensions={0} | all-to-all | bytes 524288 | tf_op jit(solution)/shard_map/all_to_all | solution.py:20
  55.4 1.2 products.1
  56.6 11.6 %all_to_all.39.in_ref = f32[2,16,72,256]{3,2,1,0:T(8,128)S(1)} all-to-all(f32[2,16,72,256]{3,2,1,0:T(8,128)S(1)} %products.1), channel_id=1, replica_groups=mesh['chip'=16,'core'=2,'col'=16] {'core'}, dimensions={0} | all-to-all | bytes 4718592 | tf_op jit(solution)/shard_map/all_to_all | solution.py:266
  68.2 0.1 sum_pair.1
  68.3 24.1 %all_to_all.40.in_ref = f32[16,72,256]{2,1,0:T(8,128)S(1)} all-to-all(f32[16,72,256]{2,1,0:T(8,128)S(1)} %sum_pair.1), channel_id=1, replica_groups=mesh['chip'=16,'core'=2,'col'=16] {'chip'}, dimensions={0} | all-to-all | bytes 2359296 | tf_op jit(solution)/shard_map/all_to_all | solution.py:267
  92.4 0.1 sum_copies.1
  92.5 19.5 %all_to_all.41.mine_ref = f32[16,72,256]{2,1,0:T(8,128)S(1)} all-to-all(f32[16,72,256]{2,1,0:T(8,128)S(1)} %sum_copies.1), channel_id=1, replica_groups=mesh['chip'=16,'core'=2,'col'=16] {'chip'}, dimensions={0} | all-to-all | bytes 2359296 | tf_op jit(solution)/shard_map/all_to_all | solution.py:267
  112.1 7.9 %inverse_factor.1.inverse_ref = f32[256,256]{1,0:T(8,128)S(1)} custom-call(f32[16,72,256]{2,1,0:T(8,128)S(1)} %all_to_all.41.mine_ref), custom_call_target="tpu_custom_call" | custom-call | tf_op jit(solution)/shard_map/inverse_factor/pallas_call | solution.py:107
  120.0 1.6 %right_and_sums.1 = (f32[896,256]{1,0:T(8,128)S(1)}, f32[32,1,256]{2,1,0:T(1,128)}) custom-call(f32[16,72,256]{2,1,0:T(8,128)S(1)} %all_to_all.41.mine_ref, f32[256,256]{1,0:T(8,128)S(1)} %inverse_factor.1.inverse_ref), custom_call_target="tpu_custom_call" | custom-call | tf_op jit(solution)/shard_map/right_and_sums/pallas_call | solution.py:150
  121.6 5.0 %collective-permute-start = (f32[896,256]{1,0:T(8,128)S(1)}, f32[896,256]{1,0:T(8,128)}, u32[]{:S(2)}, u32[]{:S(2)}) collective-permute-start(f32[896,256]{1,0:T(8,128)S(1)} %get-tuple-element.7.mine_ref), channel_id=1, source_target_pairs={{0,16},{16,0},{1,17},{17,1},{2,18},{18,2},{3,19},{19,3},{4,20},{20... | collective-permute-start | bytes 2752520 | tf_op jit(solution)/shard_map/ppermute | solution.py:273
  126.6 5.9 %all-to-all-start.5 = ((f32[32,1,256]{2,1,0:T(1,128)}), f32[32,1,256]{2,1,0:T(1,128)S(1)}, u32[]{:S(2)}, u32[]{:S(2)}) async-start(f32[32,1,256]{2,1,0:T(1,128)} %get-tuple-element.9), calls=%async_computation.5 | async-start | bytes 65536 | tf_op jit(solution)/shard_map/all_to_all | solution.py:272
  132.5 0.0 collective-permute-done.other_ref
  132.5 3.3 %feedback.1 = (bf16[256,1792]{1,0:T(8,128)(2,1)}, f32[256,256]{1,0:T(8,128)}) custom-call(s32[1]{0:T(128)} %bitcast.core_ref, f32[256,256]{1,0:T(8,128)S(1)} %bitcast.6, f32[256,256]{1,0:T(8,128)S(1)} %inverse_factor.1.inverse_ref, f32[896,256]{1,0:T(8,128)S(1)} %get-tuple-element.7.mine_ref, f32[896,256]{1,0:T(8,128)} %collective-permute-done.other_ref, ...), custom_call_target="tpu_custom_call" | custom-call | tf_op jit(solution)/shard_map/feedback/pallas_call | solution.py:194
  135.7 9.2 %all-to-all-done.5.sums_ref = f32[32,1,256]{2,1,0:T(1,128)S(1)} async-done(((f32[32,1,256]{2,1,0:T(1,128)}), f32[32,1,256]{2,1,0:T(1,128)S(1)}, u32[]{:S(2)}, u32[]{:S(2)}) %all-to-all-start.5) | async-done | bytes 32800 | tf_op jit(solution)/shard_map/all_to_all | solution.py:272
  144.9 2.3 %normalize.1 = bf16[1792,256]{1,0:T(8,128)(2,1)} custom-call(s32[1]{0:T(128)} %bitcast.core_ref, f32[896,256]{1,0:T(8,128)S(1)} %get-tuple-element.7.mine_ref, f32[896,256]{1,0:T(8,128)} %collective-permute-done.other_ref, f32[32,1,256]{2,1,0:T(1,128)S(1)} %all-to-all-done.5.sums_ref), custom_call_target="tpu_custom_call" | custom-call | tf_op jit(solution)/shard_map/normalize/pallas_call | solution.py:215
  (2 shorter events, 0.0 us)
Async XLA Ops:
  0.6 1.8 %copy-start = (bf16[1792,256]{1,0:T(8,128)(2,1)S(1)}, bf16[1792,256]{1,0:T(8,128)(2,1)}, u32[]{:S(2)}) copy-start(bf16[1792,256]{1,0:T(8,128)(2,1)} %param.5) | copy-start | bytes 2752516
  121.6 10.9 %collective-permute-start = (f32[896,256]{1,0:T(8,128)S(1)}, f32[896,256]{1,0:T(8,128)}, u32[]{:S(2)}, u32[]{:S(2)}) collective-permute-start(f32[896,256]{1,0:T(8,128)S(1)} %get-tuple-element.7.mine_ref), channel_id=1, source_target_pairs={{0,16},{16,0},{1,17},{17,1},{2,18},{18,2},{3,19},{19,3},{4,20},{20... | collective-permute-start | bytes 2752520 | tf_op jit(solution)/shard_map/ppermute | solution.py:273
  126.6 18.3 %all-to-all-start.5 = ((f32[32,1,256]{2,1,0:T(1,128)}), f32[32,1,256]{2,1,0:T(1,128)S(1)}, u32[]{:S(2)}, u32[]{:S(2)}) async-start(f32[32,1,256]{2,1,0:T(1,128)} %get-tuple-element.9), calls=%async_computation.5 | async-start | bytes 65536 | tf_op jit(solution)/shard_map/all_to_all | solution.py:272

commit v4 on v3

--- a/solution.py
+++ b/solution.py
@@ -8,16 +8,6 @@
 
 HIGHEST = lax.Precision.HIGHEST
 VMEM = pl.BlockSpec(memory_space=pltpu.VMEM)
-
-
-def scatter_sum(x, axis, count):
-    moved = lax.all_to_all(x, axis, 0, 0, tiled=True)
-    return jnp.sum(moved.reshape(count, x.shape[0] // count, x.shape[1]), axis=0)
-
-
-def gather(x, axis, count):
-    copies = jnp.broadcast_to(x[None], (count,) + x.shape).reshape(count * x.shape[0], x.shape[1])
-    return lax.all_to_all(copies, axis, 0, 0, tiled=True)
 
 
 def nt(a, b):
@@ -160,28 +150,28 @@
     )(mine, inverse)
 
 
-def sum_pair_kernel(in_ref, out_ref):
-    out_ref[...] = in_ref[0] + in_ref[1]
-
-
-def sum_pair(parts):
+def sum_pair_kernel(mine_ref, other_ref, out_ref):
+    out_ref[...] = mine_ref[...] + other_ref[...]
+
+
+def sum_pair(mine, other):
     return pl.pallas_call(
         sum_pair_kernel,
-        out_shape=jax.ShapeDtypeStruct(parts.shape[1:], parts.dtype),
-        in_specs=[VMEM],
+        out_shape=jax.ShapeDtypeStruct(mine.shape, mine.dtype),
+        in_specs=[VMEM, VMEM],
         out_specs=VMEM,
         compiler_params=pltpu.CompilerParams(vmem_limit_bytes=8 * 1024 * 1024),
         name="sum_pair",
-    )(parts)
-
-
-def feedback_kernel(core_ref, left_ref, inverse_ref, mine_ref, other_ref, blend_ref, momentum_ref, factor_ref):
+    )(mine, other)
+
+
+def feedback_kernel(left_ref, inverse_ref, mine_ref, other_ref, blend_ref, momentum_ref, factor_ref):
     factor = nt(left_ref[...], inverse_ref[...])
     factor_ref[...] = factor
     ortho = factor.astype(jnp.bfloat16)
     half = mine_ref.shape[0]
     for part in range(2):
-        right = jnp.where(core_ref[0] == part, mine_ref[...], other_ref[...])
+        right = jnp.where(lax.axis_index("core") == part, mine_ref[...], other_ref[...])
         correction = lax.dot_general(
             ortho, right.astype(jnp.bfloat16), (((1,), (1,)), ((), ())), preferred_element_type=jnp.float32
         )
@@ -190,67 +180,68 @@
         momentum_ref[:, at:at + half] = (blend - 0.1 * correction).astype(jnp.bfloat16)
 
 
-def feedback(core, left, inverse, mine, other, blend):
+def feedback(left, inverse, mine, other, blend):
     return pl.pallas_call(
         feedback_kernel,
         out_shape=(jax.ShapeDtypeStruct(blend.shape, blend.dtype), jax.ShapeDtypeStruct(left.shape, jnp.float32)),
-        in_specs=[pl.BlockSpec(memory_space=pltpu.SMEM)] + [VMEM] * 5,
+        in_specs=[VMEM] * 5,
         out_specs=(VMEM, VMEM),
         compiler_params=pltpu.CompilerParams(vmem_limit_bytes=12 * 1024 * 1024),
         cost_estimate=pl.CostEstimate(flops=0, bytes_accessed=0, transcendentals=0),
         name="feedback",
-    )(core, left, inverse, mine, other, blend)
-
-
-def normalize_kernel(core_ref, mine_ref, other_ref, sums_ref, out_ref):
+    )(left, inverse, mine, other, blend)
+
+
+def normalize_kernel(mine_ref, other_ref, sums_ref, out_ref):
     scale = lax.rsqrt(jnp.sum(sums_ref[...], axis=0) + 1e-08)
     half = mine_ref.shape[0]
     for part in range(2):
-        right = jnp.where(core_ref[0] == part, mine_ref[...], other_ref[...])
+        right = jnp.where(lax.axis_index("core") == part, mine_ref[...], other_ref[...])
         out_ref[part * half:(part + 1) * half, :] = (right * scale).astype(jnp.bfloat16)
 
 
-def normalize(core, mine, other, sums):
+def normalize(mine, other, sums):
     rows, rank = mine.shape
     return pl.pallas_call(
         normalize_kernel,
         out_shape=jax.ShapeDtypeStruct((2 * rows, rank), jnp.bfloat16),
-        in_specs=[pl.BlockSpec(memory_space=pltpu.SMEM)] + [VMEM] * 3,
+        in_specs=[VMEM] * 3,
         out_specs=VMEM,
         compiler_params=pltpu.CompilerParams(vmem_limit_bytes=8 * 1024 * 1024),
         name="normalize",
-    )(core, mine, other, sums)
-
-
-def products_kernel(left_ref, blend_ref, out_ref):
+    )(mine, other, sums)
+
+
+def products_kernel(flip, left_ref, blend_ref, out_ref):
     left = left_ref[...]
     rank = left.shape[1]
-    cores, chips = out_ref.shape[:2]
+    chips, height = out_ref.shape[:2]
+    small = rank // chips
+    large = height - small
+    half = chips * large
     gram = lax.dot_general(left, left, (((0,), (0,)), ((), ())), precision=HIGHEST, preferred_element_type=jnp.float32)
     first = left.astype(jnp.bfloat16)
     rest = left - first.astype(jnp.float32)
     second = rest.astype(jnp.bfloat16)
     third = (rest - second.astype(jnp.float32)).astype(jnp.bfloat16)
     terms = jnp.concatenate([first, second, third], axis=1)
-    half = blend_ref.shape[1] // cores
-    large, small = half // chips, rank // chips
-    for core in range(cores):
-        both = lax.dot_general(
-            blend_ref[:, core * half:(core + 1) * half], terms, (((0,), (0,)), ((), ())),
-            preferred_element_type=jnp.float32,
-        )
-        product = both[:, :rank] + both[:, rank:2 * rank] + both[:, 2 * rank:]
-        for chip in range(chips):
-            out_ref[core, chip, :large, :] = product[chip * large:(chip + 1) * large]
-            out_ref[core, chip, large:, :] = gram[chip * small:(chip + 1) * small]
-
-
-def products(left, blend, cores, chips):
+    part = 1 - lax.axis_index("core") if flip else lax.axis_index("core")
+    both = lax.dot_general(
+        blend_ref[:, pl.ds(pl.multiple_of(part * half, 128), half)], terms, (((0,), (0,)), ((), ())),
+        preferred_element_type=jnp.float32,
+    )
+    product = both[:, :rank] + both[:, rank:2 * rank] + both[:, 2 * rank:]
+    for chip in range(chips):
+        out_ref[chip, :large, :] = product[chip * large:(chip + 1) * large]
+        out_ref[chip, large:, :] = gram[chip * small:(chip + 1) * small]
+
+
+def products(flip, left, blend, chips):
     rank = left.shape[1]
-    height = blend.shape[1] // cores // chips + rank // chips
-    return pl.pallas_call(
-        products_kernel,
-        out_shape=jax.ShapeDtypeStruct((cores, chips, height, rank), jnp.float32),
+    height = blend.shape[1] // 2 // chips + rank // chips
+    return pl.pallas_call(
+        functools.partial(products_kernel, flip),
+        out_shape=jax.ShapeDtypeStruct((chips, height, rank), jnp.float32),
         in_specs=[VMEM, VMEM],
         out_specs=VMEM,
         compiler_params=pltpu.CompilerParams(vmem_limit_bytes=12 * 1024 * 1024),
@@ -259,20 +250,20 @@
 
 
 def local(chips, cores, cols, momentum, gradient, right_factor):
+    swap = [(0, 1), (1, 0)]
     blend = (momentum.astype(jnp.float32) + gradient.astype(jnp.float32)).astype(jnp.bfloat16)
     left = jnp.dot(blend, right_factor, preferred_element_type=jnp.float32)
-    left = gather(scatter_sum(left, "col", cols), "col", cols)
-
-    both = sum_pair(lax.all_to_all(products(left, blend, cores, chips), "core", 0, 0))
+    left = sum_copies(lax.all_to_all(left.reshape(cols, -1, left.shape[1]), "col", 0, 0))
+    left = lax.all_to_all(left, "col", 0, 0).reshape(blend.shape[0], -1)
+    other = lax.ppermute(products(True, left, blend, chips), "core", swap)
+    both = sum_pair(products(False, left, blend, chips), other)
     mine = lax.all_to_all(sum_copies(lax.all_to_all(both, "chip", 0, 0)), "chip", 0, 0)
     inverse = inverse_factor(mine)
-    swap = [(0, 1), (1, 0)]
-    core = lax.axis_index("core").astype(jnp.int32).reshape(1)
     right, sums = right_and_sums(mine, inverse, cores * cols)
     sums = lax.all_to_all(sums, ("core", "col"), 0, 0)
     other = lax.ppermute(right, "core", swap)
-    new_momentum, left_factor = feedback(core, left, inverse, right, other, blend)
-    new_right = normalize(core, right, other, sums)
+    new_momentum, left_factor = feedback(left, inverse, right, other, blend)
+    new_right = normalize(right, other, sums)
     return (new_momentum, new_right, left_factor)
 
 

time: 148 us -> 146 us (0.986)
  blocking collectives: 108 us -> 96.2 us
  starting transfers between devices: 10.9 us -> 19.1 us
  waiting for transfers between devices: 9.19 us -> 10.8 us
    all_to_all x3 -> x2, blocking collectives: 64.1 us -> 52.5 us  [the longest x1 28.7 us: local(): lax.all_to_all(left.reshape(cols, -1, left.shape[1]), 'col', 0, 0)]
    ppermute x0 -> x1, starting transfers between devices: none -> 8.26 us  [local(): other = lax.ppermute(products(True, left, blend, chips), 'core', swap)]
    ppermute x0 -> x1, waiting for transfers between devices: none -> 1.63 us  [local(): other = lax.ppermute(products(True, left, blend, chips), 'core', swap)]
  transfers between devices with their start and end apart: 2 -> 3, of which waited for: 1 -> 2; matrix products, arithmetic and copies ran while one was open for 0% -> 0% of each run, Pallas kernels for 2% -> 3%
where the time goes in v4:
time: 146 us
  blocking collectives  96.2 us (66%)
  starting transfers between devices  19.1 us (13%)
  Pallas kernels  17 us (12%)
  waiting for transfers between devices  10.8 us (7%)
  other arithmetic  1.75 us (1%)
    all_to_all x1, blocking collectives, local(): lax.all_to_all(left.reshape(cols, -1, left.shape[1]), 'col', 0, 0)  28.7 us
    all_to_all x1, blocking collectives, local(): lax.all_to_all(both, 'chip', 0, 0)  24.1 us
    all_to_all x1, blocking collectives, local(): left = lax.all_to_all(left, 'col', 0, 0).reshape(blend.shape[0], -1)  23.8 us
    all_to_all x1, blocking collectives, local(): lax.all_to_all(sum_copies(lax.all_to_all(both, 'chip', 0, 0)), 'chip', 0, 0)  19.5 us
    all_to_all x1, waiting for transfers between devices, local(): sums = lax.all_to_all(sums, ('core', 'col'), 0, 0)  9.19 us
    ppermute x1, starting transfers between devices, local(): other = lax.ppermute(products(True, left, blend, chips), 'core', swap)  8.26 us
    pallas_call x1, Pallas kernels, inverse_factor(): pl.pallas_call(functools.partial(inverse_factor_kernel, size, panel), out...  7.94 us
    all_to_all x1, starting transfers between devices, local(): sums = lax.all_to_all(sums, ('core', 'col'), 0, 0)  5.88 us
  transfers between devices with their start and end apart: 3, of which 2 were waited for; matrix products, arithmetic and copies ran while one was open for 0% of the time, Pallas kernels for 3%

profile of v4, /device:TPU:1, one launch (start us, length us, event | category | flops | bytes accessed | tf_op | source)
XLA Modules:
  0.0 146.0 jit_solution(11465878962675126928)
XLA Ops:
  0.6 0.0 copy-start
  0.6 1.7 %add_convert_fusion.blend_ref = bf16[256,1792]{1,0:T(8,128)(2,1)S(1)} fusion(bf16[256,1792]{1,0:T(8,128)(2,1)} %param.4, bf16[256,1792]{1,0:T(8,128)(2,1)} %param.3), kind=kLoop, calls=%fused_computation | loop fusion | flops 1835008 | bytes 2752512 | tf_op jit(solution)/shard_map/convert_element_type | solution.py:254
  2.4 0.0 copy-done
  2.4 0.4 fusion
  2.8 28.7 %all_to_all.25.in_ref = f32[16,16,256]{2,1,0:T(8,128)S(1)} all-to-all(f32[16,16,256]{2,1,0:T(8,128)S(1)} %bitcast.7), channel_id=1, replica_groups=mesh['chip'=16,'core'=2,'col'=16] {'col'}, dimensions={0} | all-to-all | bytes 524288 | tf_op jit(solution)/shard_map/all_to_all | solution.py:256
  31.5 23.8 %all_to_all.26 = f32[16,16,256]{2,1,0:T(8,128)S(1)} all-to-all(f32[16,16,256]{2,1,0:T(8,128)S(1)} %sum_copies.2), channel_id=1, replica_groups=mesh['chip'=16,'core'=2,'col'=16] {'col'}, dimensions={0} | all-to-all | bytes 524288 | tf_op jit(solution)/shard_map/all_to_all | solution.py:257
  55.4 0.8 products.3
  56.2 8.3 %collective-permute-start = (f32[16,72,256]{2,1,0:T(8,128)S(1)}, f32[16,72,256]{2,1,0:T(8,128)S(1)}, u32[]{:S(2)}, u32[]{:S(2)}) collective-permute-start(f32[16,72,256]{2,1,0:T(8,128)S(1)} %products.3), channel_id=1, source_target_pairs={{0,16},{16,0},{1,17},{17,1},{2,18},{18,2},{3,19},{19,3},{4,20},{20... | collective-permute-start | bytes 3538952 | tf_op jit(solution)/shard_map/ppermute | solution.py:258
  64.5 0.8 products.2.mine_ref
  65.3 1.6 %collective-permute-done.other_ref = f32[16,72,256]{2,1,0:T(8,128)S(1)} collective-permute-done((f32[16,72,256]{2,1,0:T(8,128)S(1)}, f32[16,72,256]{2,1,0:T(8,128)S(1)}, u32[]{:S(2)}, u32[]{:S(2)}) %collective-permute-start) | collective-permute-done | bytes 1179680 | tf_op jit(solution)/shard_map/ppermute | solution.py:258
  66.9 0.1 sum_pair.1
  67.0 24.1 %all_to_all.27.in_ref = f32[16,72,256]{2,1,0:T(8,128)S(1)} all-to-all(f32[16,72,256]{2,1,0:T(8,128)S(1)} %sum_pair.1), channel_id=1, replica_groups=mesh['chip'=16,'core'=2,'col'=16] {'chip'}, dimensions={0} | all-to-all | bytes 2359296 | tf_op jit(solution)/shard_map/all_to_all | solution.py:260
  91.2 0.1 sum_copies.3
  91.3 19.5 %all_to_all.28.mine_ref = f32[16,72,256]{2,1,0:T(8,128)S(1)} all-to-all(f32[16,72,256]{2,1,0:T(8,128)S(1)} %sum_copies.3), channel_id=1, replica_groups=mesh['chip'=16,'core'=2,'col'=16] {'chip'}, dimensions={0} | all-to-all | bytes 2359296 | tf_op jit(solution)/shard_map/all_to_all | solution.py:260
  110.8 7.9 %inverse_factor.1.inverse_ref = f32[256,256]{1,0:T(8,128)S(1)} custom-call(f32[16,72,256]{2,1,0:T(8,128)S(1)} %all_to_all.28.mine_ref), custom_call_target="tpu_custom_call" | custom-call | tf_op jit(solution)/shard_map/inverse_factor/pallas_call | solution.py:97
  118.8 1.6 %right_and_sums.1 = (f32[896,256]{1,0:T(8,128)S(1)}, f32[32,1,256]{2,1,0:T(1,128)}) custom-call(f32[16,72,256]{2,1,0:T(8,128)S(1)} %all_to_all.28.mine_ref, f32[256,256]{1,0:T(8,128)S(1)} %inverse_factor.1.inverse_ref), custom_call_target="tpu_custom_call" | custom-call | tf_op jit(solution)/shard_map/right_and_sums/pallas_call | solution.py:140
  120.3 5.0 %collective-permute-start.1 = (f32[896,256]{1,0:T(8,128)S(1)}, f32[896,256]{1,0:T(8,128)}, u32[]{:S(2)}, u32[]{:S(2)}) collective-permute-start(f32[896,256]{1,0:T(8,128)S(1)} %get-tuple-element.7.mine_ref), channel_id=1, source_target_pairs={{0,16},{16,0},{1,17},{17,1},{2,18},{18,2},{3,19},{19,3},{4,20},{20... | collective-permute-start | bytes 2752520 | tf_op jit(solution)/shard_map/ppermute | solution.py:264
  125.3 5.9 %all-to-all-start.4 = ((f32[32,1,256]{2,1,0:T(1,128)}), f32[32,1,256]{2,1,0:T(1,128)S(1)}, u32[]{:S(2)}, u32[]{:S(2)}) async-start(f32[32,1,256]{2,1,0:T(1,128)} %get-tuple-element.9), calls=%async_computation.4 | async-start | bytes 65536 | tf_op jit(solution)/shard_map/all_to_all | solution.py:263
  131.2 0.0 collective-permute-done.1.other_ref
  131.2 3.3 %feedback.1 = (bf16[256,1792]{1,0:T(8,128)(2,1)}, f32[256,256]{1,0:T(8,128)}) custom-call(f32[256,256]{1,0:T(8,128)S(1)} %bitcast.6, f32[256,256]{1,0:T(8,128)S(1)} %inverse_factor.1.inverse_ref, f32[896,256]{1,0:T(8,128)S(1)} %get-tuple-element.7.mine_ref, f32[896,256]{1,0:T(8,128)} %collective-permute-done.1.other_ref, ...), custom_call_target="tpu_custom_call" | custom-call | tf_op jit(solution)/shard_map/feedback/pallas_call | solution.py:184
  134.5 9.2 %all-to-all-done.4.sums_ref = f32[32,1,256]{2,1,0:T(1,128)S(1)} async-done(((f32[32,1,256]{2,1,0:T(1,128)}), f32[32,1,256]{2,1,0:T(1,128)S(1)}, u32[]{:S(2)}, u32[]{:S(2)}) %all-to-all-start.4) | async-done | bytes 32800 | tf_op jit(solution)/shard_map/all_to_all | solution.py:263
  143.7 2.3 %normalize.1 = bf16[1792,256]{1,0:T(8,128)(2,1)} custom-call(f32[896,256]{1,0:T(8,128)S(1)} %get-tuple-element.7.mine_ref, f32[896,256]{1,0:T(8,128)} %collective-permute-done.1.other_ref, f32[32,1,256]{2,1,0:T(1,128)S(1)} %all-to-all-done.4.sums_ref), custom_call_target="tpu_custom_call" | custom-call | tf_op jit(solution)/shard_map/normalize/pallas_call | solution.py:205
  (1 shorter events, 0.0 us)
Async XLA Ops:
  0.6 1.8 %copy-start = (bf16[1792,256]{1,0:T(8,128)(2,1)S(1)}, bf16[1792,256]{1,0:T(8,128)(2,1)}, u32[]{:S(2)}) copy-start(bf16[1792,256]{1,0:T(8,128)(2,1)} %param.5) | copy-start | bytes 2752516
  56.2 10.7 %collective-permute-start = (f32[16,72,256]{2,1,0:T(8,128)S(1)}, f32[16,72,256]{2,1,0:T(8,128)S(1)}, u32[]{:S(2)}, u32[]{:S(2)}) collective-permute-start(f32[16,72,256]{2,1,0:T(8,128)S(1)} %products.3), channel_id=1, source_target_pairs={{0,16},{16,0},{1,17},{17,1},{2,18},{18,2},{3,19},{19,3},{4,20},{20... | collective-permute-start | bytes 3538952 | tf_op jit(solution)/shard_map/ppermute | solution.py:258
  120.3 10.9 %collective-permute-start.1 = (f32[896,256]{1,0:T(8,128)S(1)}, f32[896,256]{1,0:T(8,128)}, u32[]{:S(2)}, u32[]{:S(2)}) collective-permute-start(f32[896,256]{1,0:T(8,128)S(1)} %get-tuple-element.7.mine_ref), channel_id=1, source_target_pairs={{0,16},{16,0},{1,17},{17,1},{2,18},{18,2},{3,19},{19,3},{4,20},{20... | collective-permute-start | bytes 2752520 | tf_op jit(solution)/shard_map/ppermute | solution.py:264
  125.3 18.3 %all-to-all-start.4 = ((f32[32,1,256]{2,1,0:T(1,128)}), f32[32,1,256]{2,1,0:T(1,128)S(1)}, u32[]{:S(2)}, u32[]{:S(2)}) async-start(f32[32,1,256]{2,1,0:T(1,128)} %get-tuple-element.9), calls=%async_computation.4 | async-start | bytes 65536 | tf_op jit(solution)/shard_map/all_to_all | solution.py:263

commit v5 on v4

--- a/solution.py
+++ b/solution.py
@@ -8,6 +8,10 @@
 
 HIGHEST = lax.Precision.HIGHEST
 VMEM = pl.BlockSpec(memory_space=pltpu.VMEM)
+
+
+def blend_of(momentum, gradient):
+    return (momentum.astype(jnp.float32) + gradient.astype(jnp.float32)).astype(jnp.bfloat16)
 
 
 def nt(a, b):
@@ -110,14 +114,14 @@
     total = in_ref[0]
     for index in range(1, count):
         total = total + in_ref[index]
-    for index in range(count):
+    for index in range(out_ref.shape[0]):
         out_ref[index] = total
 
 
-def sum_copies(parts):
+def sum_copies(parts, count):
     return pl.pallas_call(
         sum_copies_kernel,
-        out_shape=jax.ShapeDtypeStruct(parts.shape, parts.dtype),
+        out_shape=jax.ShapeDtypeStruct((count,) + parts.shape[1:], parts.dtype),
         in_specs=[VMEM],
         out_specs=VMEM,
         compiler_params=pltpu.CompilerParams(vmem_limit_bytes=8 * 1024 * 1024),
@@ -125,26 +129,25 @@
     )(parts)
 
 
-def right_kernel(mine_ref, inverse_ref, right_ref, sums_ref):
+def right_kernel(mine_ref, inverse_ref, first_ref, second_ref, sums_ref):
     pieces, height, rank = mine_ref.shape
-    large = right_ref.shape[0] // pieces
+    half = first_ref.shape[0]
+    large = 2 * half // pieces
     rows = mine_ref[:, :large, :].reshape(pieces * large, rank)
     right = nt(rows, inverse_ref[...])
-    right_ref[...] = right
+    first_ref[...] = right[:half]
+    second_ref[...] = right[half:]
     sums_ref[...] = jnp.broadcast_to(jnp.sum(right * right, axis=0)[None, None], sums_ref.shape)
 
 
 def right_and_sums(mine, inverse, count):
     pieces, height, rank = mine.shape
-    large = height - rank // pieces
+    part = jax.ShapeDtypeStruct((pieces * (height - rank // pieces) // 2, rank), jnp.float32)
     return pl.pallas_call(
         right_kernel,
-        out_shape=(
-            jax.ShapeDtypeStruct((pieces * large, rank), jnp.float32),
-            jax.ShapeDtypeStruct((count, 1, rank), jnp.float32),
-        ),
+        out_shape=(part, part, jax.ShapeDtypeStruct((count, 1, rank), jnp.float32)),
         in_specs=[VMEM, VMEM],
-        out_specs=(VMEM, VMEM),
+        out_specs=(VMEM, VMEM, VMEM),
         compiler_params=pltpu.CompilerParams(vmem_limit_bytes=10 * 1024 * 1024),
         name="right_and_sums",
     )(mine, inverse)
@@ -165,51 +168,53 @@
     )(mine, other)
 
 
-def feedback_kernel(left_ref, inverse_ref, mine_ref, other_ref, blend_ref, momentum_ref, factor_ref):
+def feedback_kernel(left_ref, inverse_ref, first_ref, second_ref, old_ref, gradient_ref, new_ref, factor_ref):
     factor = nt(left_ref[...], inverse_ref[...])
     factor_ref[...] = factor
     ortho = factor.astype(jnp.bfloat16)
-    half = mine_ref.shape[0]
-    for part in range(2):
-        right = jnp.where(lax.axis_index("core") == part, mine_ref[...], other_ref[...])
+    cores = first_ref.shape[0]
+    half = old_ref.shape[1] // cores
+    for core in range(cores):
+        right = jnp.concatenate([first_ref[core], second_ref[core]], axis=0)
         correction = lax.dot_general(
             ortho, right.astype(jnp.bfloat16), (((1,), (1,)), ((), ())), preferred_element_type=jnp.float32
         )
-        at = part * half
-        blend = blend_ref[:, at:at + half].astype(jnp.float32)
-        momentum_ref[:, at:at + half] = (blend - 0.1 * correction).astype(jnp.bfloat16)
-
-
-def feedback(left, inverse, mine, other, blend):
+        at = core * half
+        blend = blend_of(old_ref[:, at:at + half], gradient_ref[:, at:at + half])
+        new_ref[:, at:at + half] = (blend.astype(jnp.float32) - 0.1 * correction).astype(jnp.bfloat16)
+
+
+def feedback(left, inverse, first, second, momentum, gradient):
     return pl.pallas_call(
         feedback_kernel,
-        out_shape=(jax.ShapeDtypeStruct(blend.shape, blend.dtype), jax.ShapeDtypeStruct(left.shape, jnp.float32)),
-        in_specs=[VMEM] * 5,
+        out_shape=(jax.ShapeDtypeStruct(momentum.shape, momentum.dtype), jax.ShapeDtypeStruct(left.shape, jnp.float32)),
+        in_specs=[VMEM] * 6,
         out_specs=(VMEM, VMEM),
         compiler_params=pltpu.CompilerParams(vmem_limit_bytes=12 * 1024 * 1024),
         cost_estimate=pl.CostEstimate(flops=0, bytes_accessed=0, transcendentals=0),
         name="feedback",
-    )(left, inverse, mine, other, blend)
-
-
-def normalize_kernel(mine_ref, other_ref, sums_ref, out_ref):
+    )(left, inverse, first, second, momentum, gradient)
+
+
+def normalize_kernel(first_ref, second_ref, sums_ref, out_ref):
     scale = lax.rsqrt(jnp.sum(sums_ref[...], axis=0) + 1e-08)
-    half = mine_ref.shape[0]
-    for part in range(2):
-        right = jnp.where(lax.axis_index("core") == part, mine_ref[...], other_ref[...])
-        out_ref[part * half:(part + 1) * half, :] = (right * scale).astype(jnp.bfloat16)
-
-
-def normalize(mine, other, sums):
-    rows, rank = mine.shape
+    cores, part = first_ref.shape[:2]
+    for core in range(cores):
+        for index, source in enumerate((first_ref, second_ref)):
+            at = (2 * core + index) * part
+            out_ref[at:at + part, :] = (source[core] * scale).astype(jnp.bfloat16)
+
+
+def normalize(first, second, sums):
+    cores, part, rank = first.shape
     return pl.pallas_call(
         normalize_kernel,
-        out_shape=jax.ShapeDtypeStruct((2 * rows, rank), jnp.bfloat16),
+        out_shape=jax.ShapeDtypeStruct((2 * cores * part, rank), jnp.bfloat16),
         in_specs=[VMEM] * 3,
         out_specs=VMEM,
         compiler_params=pltpu.CompilerParams(vmem_limit_bytes=8 * 1024 * 1024),
         name="normalize",
-    )(mine, other, sums)
+    )(first, second, sums)
 
 
 def products_kernel(flip, left_ref, blend_ref, out_ref):
@@ -251,32 +256,34 @@
 
 def local(chips, cores, cols, momentum, gradient, right_factor):
     swap = [(0, 1), (1, 0)]
-    blend = (momentum.astype(jnp.float32) + gradient.astype(jnp.float32)).astype(jnp.bfloat16)
+    blend = blend_of(momentum, gradient)
     left = jnp.dot(blend, right_factor, preferred_element_type=jnp.float32)
-    left = sum_copies(lax.all_to_all(left.reshape(cols, -1, left.shape[1]), "col", 0, 0))
-    left = lax.all_to_all(left, "col", 0, 0).reshape(blend.shape[0], -1)
+    left = sum_copies(lax.all_to_all(left.reshape(cols, -1, left.shape[1]), ("near", "far"), 0, 0), cols // 2)
+    left = lax.all_to_all(left, "far", 0, 0).reshape(blend.shape[0] // 2, -1)
+    left = lax.all_gather(left, "near", tiled=True)
     other = lax.ppermute(products(True, left, blend, chips), "core", swap)
     both = sum_pair(products(False, left, blend, chips), other)
-    mine = lax.all_to_all(sum_copies(lax.all_to_all(both, "chip", 0, 0)), "chip", 0, 0)
+    mine = lax.all_to_all(sum_copies(lax.all_to_all(both, "chip", 0, 0), chips), "chip", 0, 0)
     inverse = inverse_factor(mine)
-    right, sums = right_and_sums(mine, inverse, cores * cols)
-    sums = lax.all_to_all(sums, ("core", "col"), 0, 0)
-    other = lax.ppermute(right, "core", swap)
-    new_momentum, left_factor = feedback(left, inverse, right, other, blend)
-    new_right = normalize(right, other, sums)
+    first, second, sums = right_and_sums(mine, inverse, cores * cols)
+    sums = lax.all_to_all(sums, ("core", "far", "near"), 0, 0)
+    first, second = lax.all_gather(first, "core"), lax.all_gather(second, "core")
+    new_momentum, left_factor = feedback(left, inverse, first, second, momentum, gradient)
+    new_right = normalize(first, second, sums)
     return (new_momentum, new_right, left_factor)
 
 
 def solution(mesh):
     rows, cols = mesh.devices.shape
     chips, cores = rows // 2, 2
-    split = Mesh(mesh.devices.reshape(chips, cores, cols), ("chip", "core", "col"))
+    split = Mesh(mesh.devices.reshape(chips, cores, cols // 2, 2), ("chip", "core", "far", "near"))
+    col = ("far", "near")
     row = ("chip", "core")
-    placed = (P(row, "col"), P(row, "col"), P("col", None))
+    placed = (P(row, col), P(row, col), P(col, None))
     return jax.shard_map(
         functools.partial(local, chips, cores, cols),
         mesh=split,
         in_specs=placed,
-        out_specs=(P(row, "col"), P("col", None), P(row, None)),
+        out_specs=(P(row, col), P(col, None), P(row, None)),
         check_vma=False,
     )

time: 146 us -> 144 us (0.986)
  blocking collectives: 96.2 us -> 105 us
  starting transfers between devices: 19.1 us -> 13.4 us
  waiting for transfers between devices: 10.8 us -> 6.9 us
  Pallas kernels: 17 us -> 14.5 us
    all_gather x0 -> x3, blocking collectives: none -> 9.53 us  [the longest x1 4.48 us: local(): left = lax.all_gather(left, 'near', tiled=True)]
    ppermute x1 -> x0, starting transfers between devices: 4.99 us -> none  [local(): other = lax.ppermute(right, 'core', swap)]
    all_to_all x1, waiting for transfers between devices: 9.19 us -> 5.27 us  [local(): sums = lax.all_to_all(sums, ('core', 'far', 'near'), 0, 0)]
    pallas_call x5, Pallas kernels: 7.26 us -> 4.81 us  [the longest x1 2.09 us: feedback(): pl.pallas_call(feedback_kernel, out_shape=(jax.ShapeDtypeStruct(momentum....]
    ppermute x1, starting transfers between devices: 8.26 us -> 6.72 us  [local(): other = lax.ppermute(products(True, left, blend, chips), 'core', swap)]
  transfers between devices with their start and end apart: 3 -> 2, of which waited for: 2 -> 2; matrix products, arithmetic and copies ran while one was open for 0% -> 0% of each run, Pallas kernels for 3% -> 2%
where the time goes in v5:
time: 144 us; the launch traced here: 143 us
  blocking collectives  105 us (73%)
  Pallas kernels  14.5 us (10%)
  starting transfers between devices  13.4 us (9%)
  waiting for transfers between devices  6.9 us (5%)
  other arithmetic  1.75 us (1%)
    all_to_all x1, blocking collectives, local(): lax.all_to_all(left.reshape(cols, -1, left.shape[1]), ('near', 'far'), 0, 0)  29.3 us
    all_to_all x1, blocking collectives, local(): lax.all_to_all(both, 'chip', 0, 0)  24.1 us
    all_to_all x1, blocking collectives, local(): left = lax.all_to_all(left, 'far', 0, 0).reshape(blend.shape[0] // 2, -1)  22.4 us
    all_to_all x1, blocking collectives, local(): lax.all_to_all(sum_copies(lax.all_to_all(both, 'chip', 0, 0), chips), 'ch...  19.5 us
    pallas_call x1, Pallas kernels, inverse_factor(): pl.pallas_call(functools.partial(inverse_factor_kernel, size, panel), out...  7.94 us
    ppermute x1, starting transfers between devices, local(): other = lax.ppermute(products(True, left, blend, chips), 'core', swap)  6.72 us
    all_to_all x1, starting transfers between devices, local(): sums = lax.all_to_all(sums, ('core', 'far', 'near'), 0, 0)  6.67 us
    all_to_all x1, waiting for transfers between devices, local(): sums = lax.all_to_all(sums, ('core', 'far', 'near'), 0, 0)  5.27 us
  transfers between devices with their start and end apart: 2, of which 2 were waited for; matrix products, arithmetic and copies ran while one was open for 0% of the time, Pallas kernels for 2%

profile of v5, /device:TPU:1, one launch (start us, length us, event | category | flops | bytes accessed | tf_op | source)
XLA Modules:
  0.0 143.4 jit_solution(10734314856958912046)
XLA Ops:
  0.6 0.0 copy-start
  0.6 1.7 %add_convert_fusion.blend_ref = bf16[256,1792]{1,0:T(8,128)(2,1)S(1)} fusion(bf16[256,1792]{1,0:T(8,128)(2,1)} %gradient_ref.1, bf16[256,1792]{1,0:T(8,128)(2,1)} %old_ref.1), kind=kLoop, calls=%fused_computation | loop fusion | flops 1835008 | bytes 2752512 | tf_op jit(solution)/shard_map/convert_element_type | solution.py:14
  2.4 0.0 copy-done
  2.4 0.4 fusion
  2.8 29.3 %all_to_all.25.in_ref = f32[16,16,256]{2,1,0:T(8,128)S(1)} all-to-all(f32[16,16,256]{2,1,0:T(8,128)S(1)} %bitcast.10), channel_id=1, replica_groups=mesh['chip'=16,'core'=2,'far'=8,'near'=2] {'near','far'}, dimensions={0} | all-to-all | bytes 524288 | tf_op jit(solution)/shard_map/all_to_all | solution.py:261
  32.1 22.4 %all_to_all.26 = f32[8,16,256]{2,1,0:T(8,128)S(1)} all-to-all(f32[8,16,256]{2,1,0:T(8,128)S(1)} %sum_copies.2), channel_id=1, replica_groups=mesh['chip'=16,'core'=2,'far'=8,'near'=2] {'far'}, dimensions={0} | all-to-all | bytes 262144 | tf_op jit(solution)/shard_map/all_to_all | solution.py:262
  54.5 4.5 %all_gather.15.left_ref = f32[256,256]{1,0:T(8,128)S(1)} all-gather(f32[128,256]{1,0:T(8,128)S(1)} %bitcast.11), channel_id=1, replica_groups=mesh['chip'=16,'core'=2,'far'=8,'near'=2] {'near'}, dimensions={0}, use_global_device_ids=true | all-gather | bytes 393216 | tf_op jit(solution)/shard_map/all_gather | solution.py:263
  59.0 0.8 products.3
  59.8 6.7 %collective-permute-start = (f32[16,72,256]{2,1,0:T(8,128)S(1)}, f32[16,72,256]{2,1,0:T(8,128)S(1)}, u32[]{:S(2)}, u32[]{:S(2)}) collective-permute-start(f32[16,72,256]{2,1,0:T(8,128)S(1)} %products.3), channel_id=1, source_target_pairs={{0,16},{16,0},{1,17},{17,1},{2,18},{18,2},{3,19},{19,3},{4,20},{20... | collective-permute-start | bytes 3538952 | tf_op jit(solution)/shard_map/ppermute | solution.py:264
  66.5 0.8 products.2.mine_ref
  67.4 1.6 %collective-permute-done.other_ref = f32[16,72,256]{2,1,0:T(8,128)S(1)} collective-permute-done((f32[16,72,256]{2,1,0:T(8,128)S(1)}, f32[16,72,256]{2,1,0:T(8,128)S(1)}, u32[]{:S(2)}, u32[]{:S(2)}) %collective-permute-start) | collective-permute-done | bytes 1179680 | tf_op jit(solution)/shard_map/ppermute | solution.py:264
  69.0 0.1 sum_pair.1
  69.1 24.1 %all_to_all.27.in_ref = f32[16,72,256]{2,1,0:T(8,128)S(1)} all-to-all(f32[16,72,256]{2,1,0:T(8,128)S(1)} %sum_pair.1), channel_id=1, replica_groups=mesh['chip'=16,'core'=2,'far'=8,'near'=2] {'chip'}, dimensions={0} | all-to-all | bytes 2359296 | tf_op jit(solution)/shard_map/all_to_all | solution.py:266
  93.3 0.1 sum_copies.3
  93.4 19.5 %all_to_all.28.mine_ref = f32[16,72,256]{2,1,0:T(8,128)S(1)} all-to-all(f32[16,72,256]{2,1,0:T(8,128)S(1)} %sum_copies.3), channel_id=1, replica_groups=mesh['chip'=16,'core'=2,'far'=8,'near'=2] {'chip'}, dimensions={0} | all-to-all | bytes 2359296 | tf_op jit(solution)/shard_map/all_to_all | solution.py:266
  112.9 7.9 %inverse_factor.1.inverse_ref = f32[256,256]{1,0:T(8,128)S(1)} custom-call(f32[16,72,256]{2,1,0:T(8,128)S(1)} %all_to_all.28.mine_ref), custom_call_target="tpu_custom_call" | custom-call | tf_op jit(solution)/shard_map/inverse_factor/pallas_call | solution.py:101
  120.9 1.5 %right_and_sums.1 = (f32[448,256]{1,0:T(8,128)S(1)}, f32[448,256]{1,0:T(8,128)S(1)}, f32[32,1,256]{2,1,0:T(1,128)}) custom-call(f32[16,72,256]{2,1,0:T(8,128)S(1)} %all_to_all.28.mine_ref, f32[256,256]{1,0:T(8,128)S(1)} %inverse_factor.1.inverse_ref), custom_call_target="tpu_custom_call" | custom-call | tf_op jit(solution)/shard_map/right_and_sums/pallas_call | solution.py:146
  122.4 0.0 copy-start.3
  122.4 0.8 copy-done.3
  123.2 6.7 %all-to-all-start.4 = ((f32[32,1,256]{2,1,0:T(1,128)}), f32[32,1,256]{2,1,0:T(1,128)S(1)}, u32[]{:S(2)}, u32[]{:S(2)}) async-start(f32[32,1,256]{2,1,0:T(1,128)} %get-tuple-element.11), calls=%async_computation.4 | async-start | bytes 65536 | tf_op jit(solution)/shard_map/all_to_all | solution.py:269
  129.9 0.0 copy-start.4
  129.9 0.0 copy-start.1
  129.9 0.0 copy-start.2
  129.9 2.6 %all-gather = f32[896,256]{1,0:T(8,128)S(1)} all-gather(f32[448,256]{1,0:T(8,128)S(1)} %get-tuple-element.8), channel_id=2, replica_groups=mesh['chip'=16,'core'=2,'far'=8,'near'=2] {'core'}, dimensions={0}, use_global_device_ids=true | all-gather | bytes 1376256 | tf_op jit(solution)/shard_map/all_gather | solution.py:270
  132.5 0.0 copy-done.4
  132.5 2.5 %all-gather.1 = f32[896,256]{1,0:T(8,128)S(1)} all-gather(f32[448,256]{1,0:T(8,128)S(1)} %copy-done.4), channel_id=3, replica_groups=mesh['chip'=16,'core'=2,'far'=8,'near'=2] {'core'}, dimensions={0}, use_global_device_ids=true | all-gather | bytes 1376256 | tf_op jit(solution)/shard_map/all_gather | solution.py:270
  134.9 0.0 copy-done.1
  134.9 0.0 copy-done.2
  134.9 2.1 %feedback.1 = (bf16[256,1792]{1,0:T(8,128)(2,1)}, f32[256,256]{1,0:T(8,128)}) custom-call(f32[256,256]{1,0:T(8,128)S(1)} %all_gather.15.left_ref, f32[256,256]{1,0:T(8,128)S(1)} %inverse_factor.1.inverse_ref, f32[2,448,256]{2,1,0:T(8,128)S(1)} %bitcast.6, f32[2,448,256]{2,1,0:T(8,128)S(1)} %bitcast.8, bf16[256,1792]{1,0:T(8,128)(2,1)S(1)} %copy-done.2, ...), custom_call_target="tpu_custom_call" | custom-call | tf_op jit(solution)/shard_map/feedback/pallas_call | solution.py:188
  137.0 5.3 %all-to-all-done.4.sums_ref = f32[32,1,256]{2,1,0:T(1,128)S(1)} async-done(((f32[32,1,256]{2,1,0:T(1,128)}), f32[32,1,256]{2,1,0:T(1,128)S(1)}, u32[]{:S(2)}, u32[]{:S(2)}) %all-to-all-start.4) | async-done | bytes 32800 | tf_op jit(solution)/shard_map/all_to_all | solution.py:269
  142.3 1.1 normalize.1
  (1 shorter events, 0.0 us)
Async XLA Ops:
  0.6 1.8 %copy-start = (bf16[1792,256]{1,0:T(8,128)(2,1)S(1)}, bf16[1792,256]{1,0:T(8,128)(2,1)}, u32[]{:S(2)}) copy-start(bf16[1792,256]{1,0:T(8,128)(2,1)} %param.5) | copy-start | bytes 2752516
  59.8 9.2 %collective-permute-start = (f32[16,72,256]{2,1,0:T(8,128)S(1)}, f32[16,72,256]{2,1,0:T(8,128)S(1)}, u32[]{:S(2)}, u32[]{:S(2)}) collective-permute-start(f32[16,72,256]{2,1,0:T(8,128)S(1)} %products.3), channel_id=1, source_target_pairs={{0,16},{16,0},{1,17},{17,1},{2,18},{18,2},{3,19},{19,3},{4,20},{20... | collective-permute-start | bytes 3538952 | tf_op jit(solution)/shard_map/ppermute | solution.py:264
  122.4 0.8 copy-start.3
  123.2 19.1 %all-to-all-start.4 = ((f32[32,1,256]{2,1,0:T(1,128)}), f32[32,1,256]{2,1,0:T(1,128)S(1)}, u32[]{:S(2)}, u32[]{:S(2)}) async-start(f32[32,1,256]{2,1,0:T(1,128)} %get-tuple-element.11), calls=%async_computation.4 | async-start | bytes 65536 | tf_op jit(solution)/shard_map/all_to_all | solution.py:269
  129.9 2.6 %copy-start.4 = (f32[448,256]{1,0:T(8,128)S(1)}, f32[448,256]{1,0:T(8,128)}, u32[]{:S(2)}) copy-start(f32[448,256]{1,0:T(8,128)} %copy-done.3) | copy-start | bytes 1376260
  129.9 5.1 %copy-start.1 = (bf16[256,1792]{1,0:T(8,128)(2,1)S(1)}, bf16[256,1792]{1,0:T(8,128)(2,1)}, u32[]{:S(2)}) copy-start(bf16[256,1792]{1,0:T(8,128)(2,1)} %gradient_ref.1) | copy-start | bytes 2752516
  129.9 5.1 %copy-start.2 = (bf16[256,1792]{1,0:T(8,128)(2,1)S(1)}, bf16[256,1792]{1,0:T(8,128)(2,1)}, u32[]{:S(2)}) copy-start(bf16[256,1792]{1,0:T(8,128)(2,1)} %old_ref.1) | copy-start | bytes 2752516

commit v6 on v5

--- a/solution.py
+++ b/solution.py
@@ -60,12 +60,11 @@
     return jnp.concatenate(done, axis=0)
 
 
-def inverse_factor_kernel(size, panel, mine_ref, out_ref, a_ref, y_ref):
+def inverse_factor_kernel(size, panel, gram_ref, out_ref, a_ref, y_ref):
     n = out_ref.shape[0]
-    pieces, height, _ = mine_ref.shape
     r = lax.broadcasted_iota(jnp.int32, (n, n), 0)
     c = lax.broadcasted_iota(jnp.int32, (n, n), 1)
-    gram = mine_ref[:, height - n // pieces:, :].reshape(n, n)
+    gram = gram_ref[...]
     diagonal = jnp.where(r == c, gram, 0.0)
     across = lax.rsqrt(jnp.sum(diagonal, axis=0, keepdims=True))
     down = lax.rsqrt(jnp.sum(diagonal, axis=1, keepdims=True))
@@ -96,8 +95,8 @@
             y[i] = left if lim == n else jnp.concatenate([left, y[i][:, lim:]], axis=1)
 
 
-def inverse_factor(mine, size=64, panel=16):
-    n = mine.shape[2]
+def inverse_factor(gram, size=64, panel=16):
+    n = gram.shape[0]
     return pl.pallas_call(
         functools.partial(inverse_factor_kernel, size, panel),
         out_shape=jax.ShapeDtypeStruct((n, n), jnp.float32),
@@ -106,7 +105,7 @@
         scratch_shapes=[pltpu.VMEM((n, n), jnp.float32), pltpu.VMEM((n, n), jnp.float32)],
         compiler_params=pltpu.CompilerParams(vmem_limit_bytes=8 * 1024 * 1024),
         name="inverse_factor",
-    )(mine)
+    )(gram)
 
 
 def sum_copies_kernel(in_ref, out_ref):
@@ -142,7 +141,7 @@
 
 def right_and_sums(mine, inverse, count):
     pieces, height, rank = mine.shape
-    part = jax.ShapeDtypeStruct((pieces * (height - rank // pieces) // 2, rank), jnp.float32)
+    part = jax.ShapeDtypeStruct((pieces * (height - rank // 2 // pieces) // 2, rank), jnp.float32)
     return pl.pallas_call(
         right_kernel,
         out_shape=(part, part, jax.ShapeDtypeStruct((count, 1, rank), jnp.float32)),
@@ -221,16 +220,17 @@
     left = left_ref[...]
     rank = left.shape[1]
     chips, height = out_ref.shape[:2]
-    small = rank // chips
+    small = rank // 2 // chips
     large = height - small
     half = chips * large
-    gram = lax.dot_general(left, left, (((0,), (0,)), ((), ())), precision=HIGHEST, preferred_element_type=jnp.float32)
     first = left.astype(jnp.bfloat16)
     rest = left - first.astype(jnp.float32)
     second = rest.astype(jnp.bfloat16)
     third = (rest - second.astype(jnp.float32)).astype(jnp.bfloat16)
     terms = jnp.concatenate([first, second, third], axis=1)
     part = 1 - lax.axis_index("core") if flip else lax.axis_index("core")
+    columns = left_ref[:, pl.ds(pl.multiple_of(part * (rank // 2), 128), rank // 2)]
+    gram = lax.dot_general(columns, left, (((0,), (0,)), ((), ())), precision=HIGHEST, preferred_element_type=jnp.float32)
     both = lax.dot_general(
         blend_ref[:, pl.ds(pl.multiple_of(part * half, 128), half)], terms, (((0,), (0,)), ((), ())),
         preferred_element_type=jnp.float32,
@@ -243,7 +243,7 @@
 
 def products(flip, left, blend, chips):
     rank = left.shape[1]
-    height = blend.shape[1] // 2 // chips + rank // chips
+    height = blend.shape[1] // 2 // chips + rank // 2 // chips
     return pl.pallas_call(
         functools.partial(products_kernel, flip),
         out_shape=jax.ShapeDtypeStruct((chips, height, rank), jnp.float32),
@@ -264,7 +264,9 @@
     other = lax.ppermute(products(True, left, blend, chips), "core", swap)
     both = sum_pair(products(False, left, blend, chips), other)
     mine = lax.all_to_all(sum_copies(lax.all_to_all(both, "chip", 0, 0), chips), "chip", 0, 0)
-    inverse = inverse_factor(mine)
+    rank = mine.shape[2]
+    gram = mine[:, mine.shape[1] - rank // 2 // chips:, :].reshape(rank // 2, rank)
+    inverse = inverse_factor(lax.all_gather(gram, "core", tiled=True))
     first, second, sums = right_and_sums(mine, inverse, cores * cols)
     sums = lax.all_to_all(sums, ("core", "far", "near"), 0, 0)
     first, second = lax.all_gather(first, "core"), lax.all_gather(second, "core")

time: 144 us -> 143 us (level)
  starting transfers between devices: 13.4 us -> 10.7 us
  blocking collectives: 105 us -> 107 us
    all_gather x0 -> x1, blocking collectives: none -> 4.88 us  [local(): inverse = inverse_factor(lax.all_gather(gram, 'core', tiled=True))]
    all_to_all x1, starting transfers between devices: 6.67 us -> 3.94 us  [local(): sums = lax.all_to_all(sums, ('core', 'far', 'near'), 0, 0)]
    all_to_all x1, blocking collectives: 24.1 us -> 22.5 us  [local(): lax.all_to_all(both, 'chip', 0, 0)]
where the time goes in v6:
time: 143 us; the launch traced here: 142 us
  blocking collectives  107 us (75%)
  Pallas kernels  14.3 us (10%)
  starting transfers between devices  10.7 us (7%)
  waiting for transfers between devices  6.8 us (5%)
  other arithmetic  1.75 us (1%)
    all_to_all x1, blocking collectives, local(): lax.all_to_all(left.reshape(cols, -1, left.shape[1]), ('near', 'far'), 0, 0)  29.3 us
    all_to_all x1, blocking collectives, local(): lax.all_to_all(both, 'chip', 0, 0)  22.5 us
    all_to_all x1, blocking collectives, local(): left = lax.all_to_all(left, 'far', 0, 0).reshape(blend.shape[0] // 2, -1)  22.4 us
    all_to_all x1, blocking collectives, local(): lax.all_to_all(sum_copies(lax.all_to_all(both, 'chip', 0, 0), chips), 'ch...  18.4 us
    pallas_call x1, Pallas kernels, inverse_factor(): pl.pallas_call(functools.partial(inverse_factor_kernel, size, panel), out...  7.94 us
    ppermute x1, starting transfers between devices, local(): other = lax.ppermute(products(True, left, blend, chips), 'core', swap)  6.73 us
    all_to_all x1, waiting for transfers between devices, local(): sums = lax.all_to_all(sums, ('core', 'far', 'near'), 0, 0)  5.27 us
    all_gather x1, blocking collectives, local(): inverse = inverse_factor(lax.all_gather(gram, 'core', tiled=True))  4.88 us
  transfers between devices with their start and end apart: 2, of which 2 were waited for; matrix products, arithmetic and copies ran while one was open for 0% of the time, Pallas kernels for 2%

profile of v6, /device:TPU:1, one launch (start us, length us, event | category | flops | bytes accessed | tf_op | source)
XLA Modules:
  0.0 142.4 jit_solution(5116303376243136770)
XLA Ops:
  0.6 0.0 copy-start
  0.6 1.7 %add_convert_fusion.blend_ref = bf16[256,1792]{1,0:T(8,128)(2,1)S(1)} fusion(bf16[256,1792]{1,0:T(8,128)(2,1)} %gradient_ref.1, bf16[256,1792]{1,0:T(8,128)(2,1)} %old_ref.1), kind=kLoop, calls=%fused_computation | loop fusion | flops 1835008 | bytes 2752512 | tf_op jit(solution)/shard_map/convert_element_type | solution.py:14
  2.4 0.0 copy-done
  2.4 0.4 fusion
  2.8 29.3 %all_to_all.25.in_ref = f32[16,16,256]{2,1,0:T(8,128)S(1)} all-to-all(f32[16,16,256]{2,1,0:T(8,128)S(1)} %bitcast.12), channel_id=1, replica_groups=mesh['chip'=16,'core'=2,'far'=8,'near'=2] {'near','far'}, dimensions={0} | all-to-all | bytes 524288 | tf_op jit(solution)/shard_map/all_to_all | solution.py:261
  32.1 22.4 %all_to_all.26 = f32[8,16,256]{2,1,0:T(8,128)S(1)} all-to-all(f32[8,16,256]{2,1,0:T(8,128)S(1)} %sum_copies.2), channel_id=1, replica_groups=mesh['chip'=16,'core'=2,'far'=8,'near'=2] {'far'}, dimensions={0} | all-to-all | bytes 262144 | tf_op jit(solution)/shard_map/all_to_all | solution.py:262
  54.5 4.5 %all_gather.18.left_ref = f32[256,256]{1,0:T(8,128)S(1)} all-gather(f32[128,256]{1,0:T(8,128)S(1)} %bitcast.13), channel_id=1, replica_groups=mesh['chip'=16,'core'=2,'far'=8,'near'=2] {'near'}, dimensions={0}, use_global_device_ids=true | all-gather | bytes 393216 | tf_op jit(solution)/shard_map/all_gather | solution.py:263
  59.0 0.7 products.3
  59.7 6.7 %collective-permute-start = (f32[16,64,256]{2,1,0:T(8,128)S(1)}, f32[16,64,256]{2,1,0:T(8,128)S(1)}, u32[]{:S(2)}, u32[]{:S(2)}) collective-permute-start(f32[16,64,256]{2,1,0:T(8,128)S(1)} %products.3), channel_id=1, source_target_pairs={{0,16},{16,0},{1,17},{17,1},{2,18},{18,2},{3,19},{19,3},{4,20},{20... | collective-permute-start | bytes 3145736 | tf_op jit(solution)/shard_map/ppermute | solution.py:264
  66.4 0.7 products.2.mine_ref
  67.2 1.5 %collective-permute-done.other_ref = f32[16,64,256]{2,1,0:T(8,128)S(1)} collective-permute-done((f32[16,64,256]{2,1,0:T(8,128)S(1)}, f32[16,64,256]{2,1,0:T(8,128)S(1)}, u32[]{:S(2)}, u32[]{:S(2)}) %collective-permute-start) | collective-permute-done | bytes 1048608 | tf_op jit(solution)/shard_map/ppermute | solution.py:264
  68.7 0.1 sum_pair.1
  68.8 22.5 %all_to_all.27.in_ref = f32[16,64,256]{2,1,0:T(8,128)S(1)} all-to-all(f32[16,64,256]{2,1,0:T(8,128)S(1)} %sum_pair.1), channel_id=1, replica_groups=mesh['chip'=16,'core'=2,'far'=8,'near'=2] {'chip'}, dimensions={0} | all-to-all | bytes 2097152 | tf_op jit(solution)/shard_map/all_to_all | solution.py:266
  91.3 0.1 sum_copies.3
  91.5 18.4 %all_to_all.28.mine_ref = f32[16,64,256]{2,1,0:T(8,128)S(1)} all-to-all(f32[16,64,256]{2,1,0:T(8,128)S(1)} %sum_copies.3), channel_id=1, replica_groups=mesh['chip'=16,'core'=2,'far'=8,'near'=2] {'chip'}, dimensions={0} | all-to-all | bytes 2097152 | tf_op jit(solution)/shard_map/all_to_all | solution.py:266
  109.8 4.9 %all_gather.19.gram_ref = f32[256,256]{1,0:T(8,128)S(1)} all-gather(f32[128,256]{1,0:T(8,128)S(1)} %slice_bitcast_fusion), channel_id=1, replica_groups=mesh['chip'=16,'core'=2,'far'=8,'near'=2] {'core'}, dimensions={0}, use_global_device_ids=true | all-gather | bytes 393216 | tf_op jit(solution)/shard_map/all_gather | solution.py:269
  114.7 7.9 %inverse_factor.1.inverse_ref = f32[256,256]{1,0:T(8,128)S(1)} custom-call(f32[256,256]{1,0:T(8,128)S(1)} %all_gather.19.gram_ref), custom_call_target="tpu_custom_call" | custom-call | tf_op jit(solution)/shard_map/inverse_factor/pallas_call | solution.py:100
  122.7 1.5 %right_and_sums.1 = (f32[448,256]{1,0:T(8,128)S(1)}, f32[448,256]{1,0:T(8,128)S(1)}, f32[32,1,256]{2,1,0:T(1,128)}) custom-call(f32[16,64,256]{2,1,0:T(8,128)S(1)} %all_to_all.28.mine_ref, f32[256,256]{1,0:T(8,128)S(1)} %inverse_factor.1.inverse_ref), custom_call_target="tpu_custom_call" | custom-call | tf_op jit(solution)/shard_map/right_and_sums/pallas_call | solution.py:145
  124.2 0.0 copy-start.3
  124.2 0.8 copy-done.3
  125.0 3.9 %all-to-all-start.4 = ((f32[32,1,256]{2,1,0:T(1,128)}), f32[32,1,256]{2,1,0:T(1,128)S(1)}, u32[]{:S(2)}, u32[]{:S(2)}) async-start(f32[32,1,256]{2,1,0:T(1,128)} %get-tuple-element.11), calls=%async_computation.4 | async-start | bytes 65536 | tf_op jit(solution)/shard_map/all_to_all | solution.py:271
  128.9 0.0 copy-start.4
  128.9 0.0 copy-start.1
  128.9 0.0 copy-start.2
  129.0 2.6 %all-gather = f32[896,256]{1,0:T(8,128)S(1)} all-gather(f32[448,256]{1,0:T(8,128)S(1)} %get-tuple-element.8), channel_id=2, replica_groups=mesh['chip'=16,'core'=2,'far'=8,'near'=2] {'core'}, dimensions={0}, use_global_device_ids=true | all-gather | bytes 1376256 | tf_op jit(solution)/shard_map/all_gather | solution.py:272
  131.6 0.0 copy-done.4
  131.6 2.5 %all-gather.1 = f32[896,256]{1,0:T(8,128)S(1)} all-gather(f32[448,256]{1,0:T(8,128)S(1)} %copy-done.4), channel_id=3, replica_groups=mesh['chip'=16,'core'=2,'far'=8,'near'=2] {'core'}, dimensions={0}, use_global_device_ids=true | all-gather | bytes 1376256 | tf_op jit(solution)/shard_map/all_gather | solution.py:272
  134.0 0.0 copy-done.1
  134.0 0.0 copy-done.2
  134.0 2.1 %feedback.1 = (bf16[256,1792]{1,0:T(8,128)(2,1)}, f32[256,256]{1,0:T(8,128)}) custom-call(f32[256,256]{1,0:T(8,128)S(1)} %all_gather.18.left_ref, f32[256,256]{1,0:T(8,128)S(1)} %inverse_factor.1.inverse_ref, f32[2,448,256]{2,1,0:T(8,128)S(1)} %bitcast.8, f32[2,448,256]{2,1,0:T(8,128)S(1)} %bitcast.10, bf16[256,1792]{1,0:T(8,128)(2,1)S(1)} %copy-done.2, ...), custom_call_target="tpu_custom_call" | custom-call | tf_op jit(solution)/shard_map/feedback/pallas_call | solution.py:187
  136.1 5.3 %all-to-all-done.4.sums_ref = f32[32,1,256]{2,1,0:T(1,128)S(1)} async-done(((f32[32,1,256]{2,1,0:T(1,128)}), f32[32,1,256]{2,1,0:T(1,128)S(1)}, u32[]{:S(2)}, u32[]{:S(2)}) %all-to-all-start.4) | async-done | bytes 32800 | tf_op jit(solution)/shard_map/all_to_all | solution.py:271
  141.4 1.1 normalize.1
  (2 shorter events, 0.0 us)
Async XLA Ops:
  0.6 1.8 %copy-start = (bf16[1792,256]{1,0:T(8,128)(2,1)S(1)}, bf16[1792,256]{1,0:T(8,128)(2,1)}, u32[]{:S(2)}) copy-start(bf16[1792,256]{1,0:T(8,128)(2,1)} %param.5) | copy-start | bytes 2752516
  59.7 9.0 %collective-permute-start = (f32[16,64,256]{2,1,0:T(8,128)S(1)}, f32[16,64,256]{2,1,0:T(8,128)S(1)}, u32[]{:S(2)}, u32[]{:S(2)}) collective-permute-start(f32[16,64,256]{2,1,0:T(8,128)S(1)} %products.3), channel_id=1, source_target_pairs={{0,16},{16,0},{1,17},{17,1},{2,18},{18,2},{3,19},{19,3},{4,20},{20... | collective-permute-start | bytes 3145736 | tf_op jit(solution)/shard_map/ppermute | solution.py:264
  124.2 0.8 copy-start.3
  125.0 16.4 %all-to-all-start.4 = ((f32[32,1,256]{2,1,0:T(1,128)}), f32[32,1,256]{2,1,0:T(1,128)S(1)}, u32[]{:S(2)}, u32[]{:S(2)}) async-start(f32[32,1,256]{2,1,0:T(1,128)} %get-tuple-element.11), calls=%async_computation.4 | async-start | bytes 65536 | tf_op jit(solution)/shard_map/all_to_all | solution.py:271
  128.9 2.6 %copy-start.4 = (f32[448,256]{1,0:T(8,128)S(1)}, f32[448,256]{1,0:T(8,128)}, u32[]{:S(2)}) copy-start(f32[448,256]{1,0:T(8,128)} %copy-done.3) | copy-start | bytes 1376260
  128.9 5.1 %copy-start.1 = (bf16[256,1792]{1,0:T(8,128)(2,1)S(1)}, bf16[256,1792]{1,0:T(8,128)(2,1)}, u32[]{:S(2)}) copy-start(bf16[256,1792]{1,0:T(8,128)(2,1)} %gradient_ref.1) | copy-start | bytes 2752516
  128.9 5.1 %copy-start.2 = (bf16[256,1792]{1,0:T(8,128)(2,1)S(1)}, bf16[256,1792]{1,0:T(8,128)(2,1)}, u32[]{:S(2)}) copy-start(bf16[256,1792]{1,0:T(8,128)(2,1)} %old_ref.1) | copy-start | bytes 2752516
